TPU v7x, 256 devices: a whole 4x4x8 slice. The times are simulated.
256 devices in a mesh: gy: 32 (over y, z), gz: 8 (over x, core).
Axes of the slice: x: 4, y: 4, z: 8, core: 2. Of those that a mesh axis runs over, the one named last changes fastest.
Arguments:
- grid_values: float32 [20, 256, 128, 256], P(None, 'gy', 'gz'), may hold values from -6 to 6
- spectral_weights: float32 [20, 20, 2, 32, 32, 16], P(None, None, None, 'gy', 'gz'), may hold values from -1.25 to 1.25
- bypass_weight: float32 [20, 20], replicated, may hold values from -1.25 to 1.25
- bias_vector: float32 [20], replicated, may hold values from -3 to 3
- cotangent: float32 [20, 256, 128, 256], P(None, 'gy', 'gz'), may hold values from -6 to 6
Outputs:
- output: float32 [20, 256, 128, 256], P(None, 'gy', 'gz')
- grad_values: float32 [20, 256, 128, 256], P(None, 'gy', 'gz')
- grad_weights: float32 [20, 20, 2, 32, 32, 16], P(None, None, None, 'gy', 'gz')
All inputs are finite; a program needn't handle non-finite values.
Results may differ from a plain program's by a relative error of at most 0.00011.
Values sent between devices are 32-bit elements; how exact they have to be, the bound alone decides.
No kernel may reach another device: no remote copies, remote signals or barrier semaphores. Data moves between devices by JAX's collectives and lax.ppermute only.
A program may use at most 128 MiB of HBM per device.

v0:
```python
import math

import numpy as np
import ml_dtypes

import jax
import jax.numpy as jnp
from jax import lax
from jax.experimental import pallas as pl
from jax.experimental.pallas import tpu as pltpu
from jax.sharding import PartitionSpec as P

C = 20
NX = 256
NY = 256
NZ = 128
MODES = 16
GY = 32
GZ = 8
YL = NY // GY
ZL = NZ // GZ
LANES = YL * ZL
TILES = 5
SEND_ROWS = TILES * 32
WEIGHT_ROWS = 56
GRAD_ROWS = 8
EXTRA = 748
COEF_ROWS = 768
KINDS = 40

f32 = jnp.float32
bf16 = jnp.bfloat16
VMEM_LIMIT = 8 * 1024 * 1024
WIDE_LIMIT = 16 * 1024 * 1024
FIRST_LIMIT = 62200000
DEEP_ROWS = 2 * 2 * LANES
TABLE_ROWS = DEEP_ROWS + 2 * KINDS

GROUPS = (0, 160, 320, 480)


def halves(array):
    high = array.astype(np.float32).astype(ml_dtypes.bfloat16)
    low = (array - high.astype(np.float64)).astype(np.float32).astype(ml_dtypes.bfloat16)
    return high, low


def wide_table():
    x = np.arange(NX)
    freq = np.concatenate([np.arange(16), np.arange(1, 17), [16]])
    angle = 2.0 * math.pi * ((freq[:, None] * x[None, :]) % NX) / NX
    table = np.zeros((KINDS, NX))
    table[:33] = np.cos(angle)
    table[16:32] = -np.sin(angle[16:32])
    return table


def deep_table():
    z = np.arange(NZ)
    kz = np.arange(MODES)
    angle = 2.0 * math.pi * ((kz[:, None] * z[None, :]) % NZ) / NZ
    cos, sin = np.cos(angle), np.sin(angle)
    both = np.stack([np.stack([cos, -sin], 1), np.stack([sin, cos], 1)], 0)
    both = both.reshape(2, MODES, 2, GZ, ZL)
    table = np.einsum("akrgz,yv->gakryvz", both, np.eye(YL))
    return table.reshape(GZ, 2, 2 * MODES * YL, LANES)


def lat_table():
    row = np.arange(2 * MODES)
    ky = 4 * (row % 8) + row // 8
    fy = np.where(ky < MODES, ky, ky - 2 * MODES)
    y = np.arange(NY)
    angle = 2.0 * math.pi * ((fy[:, None] * y[None, :]) % NY) / NY
    return np.concatenate([np.cos(angle), np.sin(angle)], 0)


def split(value):
    high = value.astype(bf16)
    low = (value - high.astype(f32)).astype(bf16)
    return high, low


def dot(left, right, dims=((1,), (0,))):
    return lax.dot_general(left, right, (dims, ((), ())), preferred_element_type=f32)


def dot3(left, right, dims=((1,), (0,))):
    return (
        dot(left[0], right[0], dims) + dot(left[0], right[1], dims) + dot(left[1], right[0], dims)
    )


def lane_index(shape):
    return lax.broadcasted_iota(jnp.int32, shape, len(shape) - 1)


def turn(value, amount):
    amount = amount % 128
    return value if amount == 0 else pltpu.roll(value, amount, 1)


def times_i(value):
    lane = lane_index(value.shape) % 64
    turned = jnp.where(lane < C, -turn(value, -C), turn(value, C))
    return jnp.where(lane < 2 * C, turned, 0.0)


def wide_forward(tables, values, coef_ref, channel):
    high, low = split(values)
    tall = dot(tables, high, ((1,), (1,)))
    part = tall[:KINDS] + tall[KINDS:] + dot(tables[:KINDS], low, ((1,), (1,)))
    for k, start in enumerate(GROUPS):
        coef_ref[pl.ds(start + channel, 8, stride=C), :] = part[8 * k : 8 * k + 8]
    coef_ref[pl.ds(EXTRA + channel, 1), :] = part[32:33]


def wide_inverse(coef_ref, table, channel):
    rows = [coef_ref[pl.ds(start + channel, 8, stride=C), :] for start in GROUPS]
    rows.append(coef_ref[pl.ds(EXTRA + channel, 1), :])
    rows.append(jnp.zeros((7, LANES), f32))
    coef = jnp.concatenate(rows, 0)
    high = coef.astype(bf16).astype(f32)
    stacked = jnp.concatenate([high, high, coef - high, jnp.zeros((8, LANES), f32)], 0)
    return dot(stacked.T.astype(bf16), table)


def clear_extra(coef_ref):
    coef_ref[640:EXTRA, :] = jnp.zeros((EXTRA - 640, LANES), f32)


def deep_forward(deep_ref, coef_ref, out_ref):
    def product(at, rows):
        high, low = split(rows)
        table = deep_ref[2 * LANES * at : 2 * LANES * at + 2 * LANES, :]
        return dot(table, jnp.concatenate([high, high, low], 1), ((1,), (1,)))

    real = product(0, jnp.concatenate([coef_ref[0:384, :], coef_ref[640:COEF_ROWS, :]], 0))
    imag = product(1, coef_ref[256:640, :])
    left = lane_index((2 * LANES, 128)) < 64
    tiles = (
        real[:, :128],
        real[:, 128:256],
        jnp.where(left, real[:, 256:384], imag[:, :128]),
        imag[:, 128:256],
        imag[:, 256:] - real[:, 384:],
    )
    for t, deep in enumerate(tiles):
        for g in range(GZ):
            out_ref[g, 32 * t : 32 * t + 32, :] = deep[32 * g : 32 * g + 32]


def deep_inverse(deep_ref, block_ref, coef_ref):
    def product(at, rows):
        high, low = split(rows)
        table = deep_ref[2 * LANES * at : 2 * LANES * at + 2 * LANES, : 2 * LANES]
        wide = dot(high, table)
        return wide[:, :LANES] + wide[:, LANES:] + dot(low, table[:, :LANES])

    sections = []
    for t in range(TILES):
        tile = jnp.concatenate([block_ref[g, 32 * t : 32 * t + 32, :] for g in range(GZ)], 0)
        sections.append(tile.T)
    rows = jnp.concatenate(sections, 0)
    real = product(0, jnp.concatenate([rows[:320], -rows[512:]], 0))
    coef_ref[0:320, :] = real[:320]
    coef_ref[640:COEF_ROWS, :] = real[320:]
    coef_ref[320:640, :] = product(1, rows[320:])


STEP_C = 4
STEPS = C // STEP_C


class Fetch:
    def __init__(self, sems):
        self.sems = sems
        self.count = 0

    def start(self, source, target):
        copy = pltpu.make_async_copy(source, target, self.sems.at[self.count])
        self.count += 1
        copy.start()
        return copy


def fetch_deep(fetch, deep_hbm, deep):
    return fetch.start(deep_hbm.at[lax.axis_index("gz")], deep)


def pack_weights(weights_ref, out_ref):
    units = []
    for c in range(C):
        for ky in range(4):
            for low in range(2):
                for part in range(2):
                    units.append(weights_ref[c, part * 4 + ky, pl.ds(low, GZ, stride=2), :])
    for row in range(WEIGHT_ROWS):
        pieces = units[6 * row : 6 * row + 6]
        used = C * len(pieces)
        pieces.append(jnp.zeros((GZ, 128 - used), f32))
        out_ref[:, SEND_ROWS + row, :] = jnp.concatenate(pieces, 1)


def first_kernel(
    deep_hbm, values_hbm, weights_hbm, out_ref, deep, values, weights, coef, sems
):
    fetch = Fetch(sems)
    deep_copy = fetch_deep(fetch, deep_hbm, deep)
    copies = []
    for k in range(STEPS):
        part = pl.ds(k * STEP_C, STEP_C)
        copies.append(fetch.start(values_hbm.at[part], values.at[part]))
    weights_copy = fetch.start(weights_hbm, weights)
    clear_extra(coef)
    deep_copy.wait()
    for k in range(STEPS):
        copies[k].wait()
        for channel in range(k * STEP_C, k * STEP_C + STEP_C):
            wide_forward(deep[DEEP_ROWS:, :NX], values[channel], coef, channel)
    weights_copy.wait()
    pack_weights(weights, out_ref)
    deep_forward(deep, coef, out_ref)


def anywhere():
    return pl.BlockSpec(memory_space=pl.ANY)


def vmem():
    return pl.BlockSpec(memory_space=pltpu.VMEM)


def params(limit=VMEM_LIMIT):
    return pltpu.CompilerParams(vmem_limit_bytes=limit)


def deep_scratch():
    return pltpu.VMEM((TABLE_ROWS, 3 * LANES), bf16)


def first_call(deep, values, weights):
    shape = (GZ, SEND_ROWS + WEIGHT_ROWS, 128)
    return pl.pallas_call(
        first_kernel,
        in_specs=[anywhere()] * 3,
        out_specs=vmem(),
        out_shape=jax.ShapeDtypeStruct(shape, f32),
        scratch_shapes=[
            deep_scratch(),
            pltpu.VMEM(values.shape, f32),
            pltpu.VMEM(weights.shape, f32),
            pltpu.VMEM((COEF_ROWS, LANES), f32),
            pltpu.SemaphoreType.DMA((STEPS + 2,)),
        ],
        compiler_params=params(FIRST_LIMIT),
    )(deep, values, weights)


def join_kernel(block_ref, out_ref):
    tiles = []
    for t in range(TILES):
        rows = slice(32 * t, 32 * t + 32)
        total = block_ref[0, rows, :]
        for g in range(1, GZ):
            total = total + block_ref[g, rows, :]
        tiles.append(total)
    joined = jnp.concatenate(tiles, 1)
    gap = jnp.zeros((YL, 64 - 2 * C), f32)

    def arranged(at):
        cut = joined[:, C * at : C * at + C]
        return jnp.concatenate([cut[0:8], cut[8:16], gap, cut[16:24], cut[24:32], gap], 1)

    out_ref[0:8, :] = arranged(0)
    for f in range(1, 16):
        real = arranged(f)
        imag = arranged(15 + f)
        out_ref[8 * f : 8 * f + 8, :] = real + imag
        out_ref[8 * (32 - f) : 8 * (32 - f) + 8, :] = real - imag
    out_ref[128:136, :] = -arranged(31)


def join_call(block):
    return pl.pallas_call(
        join_kernel,
        in_specs=[vmem()],
        out_specs=vmem(),
        out_shape=jax.ShapeDtypeStruct((NY, 128), f32),
        compiler_params=params(),
    )(block)


def fork_blocks(block_ref, out_ref):
    blocks = [block_ref[0:8, :]]
    differences = []
    for f in range(1, 16):
        plus = block_ref[8 * f : 8 * f + 8, :]
        minus = block_ref[8 * (32 - f) : 8 * (32 - f) + 8, :]
        blocks.append(plus + minus)
        differences.append(plus - minus)
    blocks = blocks + differences + [-block_ref[128:136, :]]
    for k in range(4):
        lane = 64 * (k // 2) + C * (k % 2)
        row = jnp.concatenate([b[:, lane : lane + C] for b in blocks], 1)
        for t in range(TILES):
            piece = row[:, 128 * t : 128 * t + 128]
            for g in range(GZ):
                out_ref[g, 32 * t + 8 * k : 32 * t + 8 * k + 8, :] = piece


def fork_kernel(block_ref, out_ref):
    fork_blocks(block_ref, out_ref)


def fork_grads_kernel(block_ref, modes_ref, grad_ref, out_ref):
    fork_blocks(block_ref, out_ref)
    for ky in range(4):
        out_ref[:, SEND_ROWS + ky, :] = modes_ref[8 * ky : 8 * ky + 8, :]
        out_ref[:, SEND_ROWS + 4 + ky, :] = grad_ref[8 * ky : 8 * ky + 8, :]


def fork_call(block, *grads):
    rows = SEND_ROWS + (GRAD_ROWS if grads else 0)
    return pl.pallas_call(
        fork_grads_kernel if grads else fork_kernel,
        in_specs=[vmem()] * (1 + len(grads)),
        out_specs=vmem(),
        out_shape=jax.ShapeDtypeStruct((GZ, rows, 128), f32),
        compiler_params=params(),
    )(block, *grads)


def unpack(block_ref, c):
    left = lane_index((GZ, 128)) < 64
    rows = []
    for ky in range(4):
        sides = []
        for low in range(2):
            unit = (c * 4 + ky) * 2 + low
            side = block_ref[:, SEND_ROWS + unit // 3, :]
            sides.append(turn(side, 64 * low - 40 * (unit % 3)))
        rows.append(jnp.where(left, sides[0], sides[1]))
    return jnp.concatenate(rows, 0)


def lat_forward(lat, block):
    both = dot3(lat, split(block))
    return both[:32] - times_i(both[32:])


def lat_inverse(lat_back, modes):
    return dot3(lat_back, split(jnp.concatenate([modes, times_i(modes)], 0)))


def spread(modes, lane):
    left = lane_index(modes.shape) < 64
    return jnp.where(left, modes[:, lane : lane + 1], modes[:, 64 + lane : 65 + lane])


SCALING = 1.0 / math.sqrt(NX * NY * NZ)


def depth_factor():
    lane = lane_index((32, 128))
    first = (lane < 64) & (lax.axis_index("gz") == 0)
    scale = 1.0 / (2.0 * math.sqrt(4.0 * MODES * MODES * MODES))
    factor = jnp.where(first, f32(scale), f32(2.0 * scale))
    return jnp.where(lane % 64 < 2 * C, factor, 0.0)


def mix_kernel(
    lat_h, lat_l, back_h, back_l, block_ref, first_ref, out_ref, modes_ref, weights_ref
):
    modes = lat_forward((lat_h[...], lat_l[...]), block_ref[...]) * SCALING
    modes_ref[...] = modes
    direct = jnp.zeros((32, 128), f32)
    crossed = jnp.zeros((32, 128), f32)
    for c in range(C):
        weight = unpack(first_ref, c)
        weights_ref[c] = weight
        direct = direct + spread(modes, c) * weight
        crossed = crossed + spread(modes, C + c) * weight
    mixed = (direct + times_i(crossed)) * depth_factor()
    out_ref[...] = lat_inverse((back_h[...], back_l[...]), mixed)


def mix_call(lat, block, first):
    return pl.pallas_call(
        mix_kernel,
        in_specs=[vmem()] * 6,
        out_specs=[vmem()] * 3,
        out_shape=[
            jax.ShapeDtypeStruct((NY, 128), f32),
            jax.ShapeDtypeStruct((32, 128), f32),
            jax.ShapeDtypeStruct((C, 32, 128), f32),
        ],
        compiler_params=params(),
    )(*lat, block, first)


def join_table():
    table = np.zeros((C, 2, 128, 128))
    for c in range(C):
        for part in range(2):
            for low in range(2):
                table[c, part, 64 * low : 64 * low + 2 * C, 64 * low + C * part + c] = 1
    return table.reshape(2 * 128 * C, 128)


def adjoint_kernel(
    lat_h, lat_l, back_h, back_l, join_ref, block_ref, weights_ref, out_ref, grad_ref
):
    grad = lat_forward((lat_h[...], lat_l[...]), block_ref[...]) * depth_factor()
    grad_ref[...] = grad
    crossed = -times_i(grad)
    terms = []
    for c in range(C):
        weight = weights_ref[c]
        terms += [weight * grad, weight * crossed]
    high, low = split(jnp.concatenate(terms, 1))
    both = dot(jnp.concatenate([high, low], 0), join_ref[...])
    block = both[:32] + both[32:]
    out_ref[...] = lat_inverse((back_h[...], back_l[...]), block * SCALING)


def adjoint_call(lat, joins, block, weights):
    return pl.pallas_call(
        adjoint_kernel,
        in_specs=[vmem()] * 7,
        out_specs=[vmem()] * 2,
        out_shape=[
            jax.ShapeDtypeStruct((NY, 128), f32),
            jax.ShapeDtypeStruct((32, 128), f32),
        ],
        compiler_params=params(),
    )(*lat, joins, block, weights)


ROOT = math.sqrt(2.0 / math.pi)
CUBE = 0.044715


def bypass_blocks(bypass, dims):
    row = lax.broadcasted_iota(jnp.int32, (8 * C, C), 0)
    column = lax.broadcasted_iota(jnp.int32, (8 * C, C), 1)
    select = (row // 8 == column).astype(f32).astype(bf16)
    row = lax.broadcasted_iota(jnp.int32, (8 * C, 8 * C), 0)
    column = lax.broadcasted_iota(jnp.int32, (8 * C, 8 * C), 1)
    same = row % 8 == column % 8
    blocks = []
    for half in split(bypass):
        wide = dot(dot(select, half, dims).astype(bf16), select, ((1,), (1,)))
        blocks.append(jnp.where(same, wide, 0.0))
    return jnp.concatenate(blocks, 0).astype(bf16)


def bypass_product(blocks, values):
    high, low = split(values)
    tall = dot(blocks, high)
    return tall[: 8 * C] + tall[8 * C :] + dot(blocks[: 8 * C], low)


def layer_kernel(
    back_ref, deep_hbm, bypass_hbm, bias_hbm, block_ref, values_hbm, cot_hbm,
    out_hbm, slope_hbm, send_ref, deep, bypass, bias, values, cots, field, coef, blocks,
    small_sems, value_sems, cot_sems, out_sems, slope_sems
):
    fetch = Fetch(small_sems)
    deep_copy = fetch_deep(fetch, deep_hbm, deep)
    bypass_copy = fetch.start(bypass_hbm, bypass)
    bias_copy = fetch.start(bias_hbm, bias)

    def value_copy(y):
        return pltpu.make_async_copy(values_hbm.at[:, y], values.at[:, y], value_sems.at[y])

    def cot_copy(y):
        return pltpu.make_async_copy(cot_hbm.at[:, y], cots.at[:, y], cot_sems.at[y])

    def out_copy(y):
        return pltpu.make_async_copy(values.at[:, y], out_hbm.at[:, y], out_sems.at[y])

    def slope_copy(y):
        return pltpu.make_async_copy(cots.at[:, y], slope_hbm.at[:, y], slope_sems.at[y])

    for y in range(YL):
        value_copy(y).start()
        cot_copy(y).start()
    deep_copy.wait()
    deep_inverse(deep, block_ref, coef)
    bypass_copy.wait()
    blocks[...] = bypass_blocks(bypass[...], ((1,), (1,)))
    bias_copy.wait()
    for channel in range(C):
        field[channel] = wide_inverse(coef, back_ref[...], channel) + bias[channel]

    @pl.loop(0, YL)
    def _(y):
        value_copy(y).wait()
        cot_copy(y).wait()
        for half in range(2):
            rows = pl.ds(8 * half, 8)
            place = pl.ds(pl.multiple_of(y * ZL + 8 * half, 8), 8)
            before = bypass_product(
                blocks[...], values[:, y, rows, :].reshape(8 * C, NX)
            ) + field[:, place, :].reshape(8 * C, NX)
            square = before * before
            bend = jnp.tanh(before * (ROOT + (ROOT * CUBE) * square))
            half_up = 0.5 + 0.5 * bend
            rate = half_up + (half_up - half_up * half_up) * before * (
                2.0 * ROOT + (6.0 * ROOT * CUBE) * square
            )
            cot = cots[:, y, rows, :].reshape(8 * C, NX)
            values[:, y, rows, :] = (before * half_up).reshape(C, 8, NX)
            cots[:, y, rows, :] = (cot * rate).reshape(C, 8, NX)
        out_copy(y).start()
        slope_copy(y).start()

    clear_extra(coef)
    for channel in range(C):
        wide_forward(deep[DEEP_ROWS:, :NX], cots[channel].reshape(LANES, NX), coef, channel)
    deep_forward(deep, coef, send_ref)
    for y in range(YL):
        out_copy(y).wait()
        slope_copy(y).wait()


def grid_buffer():
    return pltpu.VMEM((C, YL, ZL, NX), f32)


def layer_call(back, deep, bypass, bias, block, values, cotangent):
    grid_shape = jax.ShapeDtypeStruct((C, YL, ZL, NX), f32)
    many = pltpu.SemaphoreType.DMA((YL,))
    return pl.pallas_call(
        layer_kernel,
        in_specs=[vmem(), anywhere(), anywhere(), anywhere(), vmem()]
        + [anywhere()] * 2,
        out_specs=[anywhere(), anywhere(), vmem()],
        out_shape=[
            grid_shape,
            grid_shape,
            jax.ShapeDtypeStruct((GZ, SEND_ROWS, 128), f32),
        ],
        scratch_shapes=[
            deep_scratch(),
            pltpu.VMEM((C, C), f32),
            pltpu.SMEM((C,), f32),
            grid_buffer(),
            grid_buffer(),
            pltpu.VMEM((C, LANES, NX), f32),
            pltpu.VMEM((COEF_ROWS, LANES), f32),
            pltpu.VMEM((16 * C, 8 * C), bf16),
            pltpu.SemaphoreType.DMA((3,)),
            many,
            many,
            many,
            many,
        ],
        compiler_params=params(WIDE_LIMIT),
    )(back, deep, bypass, bias, block, values, cotangent)


def last_kernel(
    back_ref, deep_hbm, bypass_hbm, block_ref, slope_hbm, out_hbm, weight_hbm, deep, bypass,
    slopes, field, coef, blocks, weight, modes_rows, grad_rows, small_sems, slope_sems, out_sems
):
    fetch = Fetch(small_sems)
    deep_copy = fetch_deep(fetch, deep_hbm, deep)
    bypass_copy = fetch.start(bypass_hbm, bypass)

    def slope_copy(y):
        return pltpu.make_async_copy(slope_hbm.at[:, y], slopes.at[:, y], slope_sems.at[y])

    def out_copy(y):
        return pltpu.make_async_copy(slopes.at[:, y], out_hbm.at[:, y], out_sems.at[y])

    for y in range(YL):
        slope_copy(y).start()
    for ky in range(4):
        for low in range(2):
            rows = pl.ds(low, GZ, stride=2)
            modes_rows[rows, :] = turn(block_ref[:, SEND_ROWS + ky, :], 64 * low)
            grad_rows[rows, :] = turn(block_ref[:, SEND_ROWS + 4 + ky, :], 64 * low)
        modes = modes_rows[...]
        grad_real = grad_rows[...]
        grad_imag = turn(grad_real, -C)
        for channel in range(C):
            real = modes[:, channel : channel + 1]
            imag = modes[:, C + channel : C + channel + 1]
            weight[channel, ky] = (real * grad_real + imag * grad_imag)[:, :C]
            weight[channel, 4 + ky] = (real * grad_imag - imag * grad_real)[:, :C]
    weight_copy = fetch.start(weight, weight_hbm)
    deep_copy.wait()
    deep_inverse(deep, block_ref, coef)
    bypass_copy.wait()
    blocks[...] = bypass_blocks(bypass[...], ((1,), (0,)))
    for channel in range(C):
        field[channel] = wide_inverse(coef, back_ref[...], channel)

    @pl.loop(0, YL)
    def _(y):
        slope_copy(y).wait()
        for half in range(2):
            rows = pl.ds(8 * half, 8)
            place = pl.ds(pl.multiple_of(y * ZL + 8 * half, 8), 8)
            total = bypass_product(
                blocks[...], slopes[:, y, rows, :].reshape(8 * C, NX)
            ) + field[:, place, :].reshape(8 * C, NX)
            slopes[:, y, rows, :] = total.reshape(C, 8, NX)
        out_copy(y).start()

    for y in range(YL):
        out_copy(y).wait()
    weight_copy.wait()


def last_call(back, deep, bypass, block, slopes):
    weight_shape = (C, 8, MODES, C)
    many = pltpu.SemaphoreType.DMA((YL,))
    return pl.pallas_call(
        last_kernel,
        in_specs=[vmem(), anywhere(), anywhere(), vmem(), anywhere()],
        out_specs=[anywhere(), anywhere()],
        out_shape=[
            jax.ShapeDtypeStruct((C, YL, ZL, NX), f32),
            jax.ShapeDtypeStruct(weight_shape, f32),
        ],
        scratch_shapes=[
            deep_scratch(),
            pltpu.VMEM((C, C), f32),
            grid_buffer(),
            pltpu.VMEM((C, LANES, NX), f32),
            pltpu.VMEM((COEF_ROWS, LANES), f32),
            pltpu.VMEM((16 * C, 8 * C), bf16),
            pltpu.VMEM(weight_shape, f32),
            pltpu.VMEM((MODES, 128), f32),
            pltpu.VMEM((MODES, 128), f32),
            pltpu.SemaphoreType.DMA((3,)),
            many,
            many,
        ],
        compiler_params=params(WIDE_LIMIT),
    )(back, deep, bypass, block, slopes)


def exchange(block, axis):
    return lax.all_to_all(block, axis, split_axis=0, concat_axis=0, tiled=True)


def over_y(rows):
    return exchange(rows.reshape(GY, YL, 128), "gy").reshape(NY, 128)


def shards(grid_values, spectral_weights, bypass_weight, bias_vector, cotangent):
    wide_high, wide_low = halves(wide_table())
    nothing = np.zeros((8, NX), ml_dtypes.bfloat16)
    back = jnp.asarray(np.concatenate([wide_high, wide_low, wide_high, nothing], 0))
    deep_high, deep_low = halves(deep_table())
    deep = np.concatenate([deep_high, deep_low, deep_high], 3).reshape(GZ, DEEP_ROWS, 3 * LANES)
    wide = np.concatenate([wide_high, wide_low], 0)
    wide = np.concatenate([wide, np.zeros((2 * KINDS, LANES), ml_dtypes.bfloat16)], 1)
    deep = np.concatenate([deep, np.broadcast_to(wide, (GZ,) + wide.shape)], 1)
    deep = jnp.asarray(deep)
    joins = jnp.asarray(join_table().astype(ml_dtypes.bfloat16))
    lat_full = lat_table()
    lat = tuple(jnp.asarray(t) for t in halves(lat_full) + halves(lat_full.T.copy()))
    weights = jnp.transpose(spectral_weights, (0, 2, 3, 4, 5, 1)).reshape(C, 8, MODES, C)
    values = grid_values.reshape(C, LANES, NX)

    first = exchange(first_call(deep, values, weights), "gz")
    rows, modes, mixing = mix_call(lat, over_y(join_call(first)), first)
    got = exchange(fork_call(over_y(rows)), "gz")
    output, slopes, sent = layer_call(
        back, deep, bypass_weight, bias_vector, got, grid_values, cotangent
    )

    got = exchange(sent, "gz")
    rows, grad = adjoint_call(lat, joins, over_y(join_call(got)), mixing)
    got = exchange(fork_call(over_y(rows), modes, grad), "gz")
    grad_values, weight_grad = last_call(back, deep, bypass_weight, got, slopes)
    weight_grad = weight_grad.reshape(C, 2, 1, 4, MODES, C)
    return output, grad_values, jnp.transpose(weight_grad, (0, 5, 1, 2, 3, 4))


def solution(mesh):
    in_specs = (
        P(None, "gy", "gz", None),
        P(None, None, None, "gy", "gz", None),
        P(),
        P(),
        P(None, "gy", "gz", None),
    )
    out_specs = (
        P(None, "gy", "gz", None),
        P(None, "gy", "gz", None),
        P(None, None, None, "gy", "gz", None),
    )
    return jax.shard_map(shards, mesh=mesh, in_specs=in_specs, out_specs=out_specs, check_vma=False)
```

profile of v0, /device:TPU:1, one launch (start us, length us, event | category | flops | bytes accessed | tf_op | source)
XLA Modules:
  0.0 147.6 jit_solution(8474355408883201497)
XLA Ops:
  0.6 0.0 copy-start.2
  0.6 4.4 %shard_map.139 = f32[8,216,128]{2,1,0:T(8,128)} custom-call(bf16[8,592,384]{2,1,0:T(8,128)(2,1)} %constant.15.clone.deep_hbm, f32[20,128,256]{2,1,0:T(8,128)} %bitcast.17, f32[20,8,16,20]{3,2,1,0:T(8,128)} %bitcast.26), custom_call_target="tpu_custom_call" | custom-call | tf_op jit(solution)/shard_map/pallas_call | solution.py:244
  5.0 0.0 copy-start.4
  5.0 0.0 copy-start.5
  5.0 0.0 copy-start.7
  5.0 0.0 copy-start.8
  5.1 0.0 copy-start.1
  5.1 20.4 %all_to_all.40.block_ref.first_ref = f32[8,216,128]{2,1,0:T(8,128)S(1)} all-to-all(f32[8,216,128]{2,1,0:T(8,128)} %shard_map.139), channel_id=1, replica_groups=mesh['gy'=32,'gz'=8] {'gz'}, dimensions={0} | all-to-all | bytes 1769472 | tf_op jit(solution)/shard_map/all_to_all | solution.py:648
  25.5 0.0 copy-start
  25.5 0.0 copy-start.6
  25.5 0.0 copy-start.9
  25.5 0.0 copy-start.10
  25.5 0.2 shard_map.140
  25.8 19.5 %all_to_all.41 = f32[32,8,128]{2,1,0:T(8,128)S(1)} all-to-all(f32[32,8,128]{2,1,0:T(8,128)S(1)} %bitcast.22), channel_id=1, replica_groups=mesh['gy'=32,'gz'=8] {'gy'}, dimensions={0} | all-to-all | bytes 262144 | tf_op jit(solution)/shard_map/all_to_all | solution.py:648
  45.3 0.0 copy-done.4
  45.3 0.0 copy-done.5
  45.3 0.0 copy-done.7
  45.3 0.0 copy-done.8
  45.3 1.2 shard_map.141
  46.5 12.7 %all_to_all.42 = f32[32,8,128]{2,1,0:T(8,128)S(1)} all-to-all(f32[32,8,128]{2,1,0:T(8,128)S(1)} %bitcast.25), channel_id=1, replica_groups=mesh['gy'=32,'gz'=8] {'gy'}, dimensions={0} | all-to-all | bytes 262144 | tf_op jit(solution)/shard_map/all_to_all | solution.py:648
  59.3 0.2 shard_map.142
  59.5 16.8 %all_to_all.43.block_ref = f32[8,160,128]{2,1,0:T(8,128)S(1)} all-to-all(f32[8,160,128]{2,1,0:T(8,128)S(1)} %shard_map.142), channel_id=1, replica_groups=mesh['gy'=32,'gz'=8] {'gz'}, dimensions={0} | all-to-all | bytes 1310720 | tf_op jit(solution)/shard_map/all_to_all | solution.py:648
  76.2 0.0 copy-done.2
  76.2 0.0 copy-done.1
  76.2 0.0 copy-done
  76.2 0.0 copy-done.6
  76.2 0.0 copy-done.9
  76.3 0.0 copy-done.10
  76.3 7.6 %shard_map.143 = (f32[20,8,16,256]{3,2,1,0:T(8,128)}, f32[20,8,16,256]{3,2,1,0:T(8,128)S(1)}, f32[8,160,128]{2,1,0:T(8,128)S(1)}) custom-call(bf16[128,256]{1,0:T(8,128)(2,1)S(1)} %copy-done.6, bf16[8,592,384]{2,1,0:T(8,128)(2,1)S(1)} %copy-done, f32[20,20]{1,0:T(8,128)S(1)} %copy-done.9, f32[20]{0:T(128)S(1)} %copy-done.10, ...), custom_call_target="tpu_custom_call" | custom-call | tf_op jit(solution)/shard_map/pallas_call | solution.py:535
  83.9 0.0 copy-start.3
  83.9 14.3 %all_to_all.44.block_ref = f32[8,160,128]{2,1,0:T(8,128)S(1)} all-to-all(f32[8,160,128]{2,1,0:T(8,128)S(1)} %get-tuple-element.15), channel_id=1, replica_groups=mesh['gy'=32,'gz'=8] {'gz'}, dimensions={0} | all-to-all | bytes 1310720 | tf_op jit(solution)/shard_map/all_to_all | solution.py:648
  98.2 0.2 shard_map.144
  98.5 12.4 %all_to_all.45 = f32[32,8,128]{2,1,0:T(8,128)S(1)} all-to-all(f32[32,8,128]{2,1,0:T(8,128)S(1)} %bitcast.21), channel_id=1, replica_groups=mesh['gy'=32,'gz'=8] {'gy'}, dimensions={0} | all-to-all | bytes 262144 | tf_op jit(solution)/shard_map/all_to_all | solution.py:648
  110.8 0.0 copy-done.3
  110.8 0.9 shard_map.145
  111.7 12.7 %all_to_all.46 = f32[32,8,128]{2,1,0:T(8,128)S(1)} all-to-all(f32[32,8,128]{2,1,0:T(8,128)S(1)} %bitcast.24), channel_id=1, replica_groups=mesh['gy'=32,'gz'=8] {'gy'}, dimensions={0} | all-to-all | bytes 262144 | tf_op jit(solution)/shard_map/all_to_all | solution.py:648
  124.4 0.2 shard_map.146
  124.6 17.2 %all_to_all.47.block_ref = f32[8,168,128]{2,1,0:T(8,128)S(1)} all-to-all(f32[8,168,128]{2,1,0:T(8,128)S(1)} %shard_map.146), channel_id=1, replica_groups=mesh['gy'=32,'gz'=8] {'gz'}, dimensions={0} | all-to-all | bytes 1376256 | tf_op jit(solution)/shard_map/all_to_all | solution.py:648
  141.8 5.7 %shard_map.147 = (f32[20,8,16,256]{3,2,1,0:T(8,128)}, f32[20,8,16,20]{3,2,1,0:T(8,128)}) custom-call(bf16[128,256]{1,0:T(8,128)(2,1)S(1)} %copy-done.6, bf16[8,592,384]{2,1,0:T(8,128)(2,1)S(1)} %copy-done, f32[20,20]{1,0:T(8,128)S(1)} %copy-done.9, f32[8,168,128]{2,1,0:T(8,128)S(1)} %all_to_all.47.block_ref, f32[20,8,16,256]{3,2,1,0:T(8,128)S(1)} %get-tuple-element.20.slope_hbm), custom_call_target="tpu_custom_call" | custom-call | tf_op jit(solution)/shard_map/pallas_call | solution.py:621
Async XLA Ops:
  0.6 75.6 %copy-start.2 = (f32[20,8,16,256]{3,2,1,0:T(8,128)S(1)}, f32[20,8,16,256]{3,2,1,0:T(8,128)}, u32[]{:S(2)}) copy-start(f32[20,8,16,256]{3,2,1,0:T(8,128)} %cot_hbm.1) | copy-start | bytes 7864324
  5.0 40.3 %copy-start.4 = (bf16[256,64]{1,0:T(8,128)(2,1)S(1)}, bf16[256,64]{1,0:T(8,128)(2,1)}, u32[]{:S(2)}) copy-start(bf16[256,64]{1,0:T(8,128)(2,1)} %constant.20.clone.back_l) | copy-start | bytes 98308
  5.0 40.3 %copy-start.5 = (bf16[256,64]{1,0:T(8,128)(2,1)S(1)}, bf16[256,64]{1,0:T(8,128)(2,1)}, u32[]{:S(2)}) copy-start(bf16[256,64]{1,0:T(8,128)(2,1)} %constant.19.clone.back_h) | copy-start | bytes 98308
  5.0 40.3 %copy-start.7 = (bf16[64,256]{1,0:T(8,128)(2,1)S(1)}, bf16[64,256]{1,0:T(8,128)(2,1)}, u32[]{:S(2)}) copy-start(bf16[64,256]{1,0:T(8,128)(2,1)} %constant.18.clone.lat_l) | copy-start | bytes 98308
  5.0 40.3 %copy-start.8 = (bf16[64,256]{1,0:T(8,128)(2,1)S(1)}, bf16[64,256]{1,0:T(8,128)(2,1)}, u32[]{:S(2)}) copy-start(bf16[64,256]{1,0:T(8,128)(2,1)} %constant.17.clone.lat_h) | copy-start | bytes 98308
  5.1 71.2 %copy-start.1 = (f32[20,8,16,256]{3,2,1,0:T(8,128)S(1)}, f32[20,8,16,256]{3,2,1,0:T(8,128)}, u32[]{:S(2)}) copy-start(f32[20,8,16,256]{3,2,1,0:T(8,128)} %values_hbm.1) | copy-start | bytes 7864324
  25.5 50.7 %copy-start = (bf16[8,592,384]{2,1,0:T(8,128)(2,1)S(1)}, bf16[8,592,384]{2,1,0:T(8,128)(2,1)}, u32[]{:S(2)}) copy-start(bf16[8,592,384]{2,1,0:T(8,128)(2,1)} %constant.15.clone.deep_hbm) | copy-start | bytes 10911748
  25.5 50.7 %copy-start.6 = (bf16[128,256]{1,0:T(8,128)(2,1)S(1)}, bf16[128,256]{1,0:T(8,128)(2,1)}, u32[]{:S(2)}) copy-start(bf16[128,256]{1,0:T(8,128)(2,1)} %constant.14.clone.back_ref) | copy-start | bytes 196612
  25.5 50.7 %copy-start.9 = (f32[20,20]{1,0:T(8,128)S(1)}, f32[20,20]{1,0:T(8,128)}, u32[]{:S(2)}) copy-start(f32[20,20]{1,0:T(8,128)} %bypass_hbm.3) | copy-start | bytes 4804
  25.5 50.7 %copy-start.10 = (f32[20]{0:T(128)S(1)}, f32[20]{0:T(128)}, u32[]{:S(2)}) copy-start(f32[20]{0:T(128)} %bias_hbm.1) | copy-start | bytes 244
  83.9 26.9 %copy-start.3 = (bf16[5120,128]{1,0:T(8,128)(2,1)S(1)}, bf16[5120,128]{1,0:T(8,128)(2,1)}, u32[]{:S(2)}) copy-start(bf16[5120,128]{1,0:T(8,128)(2,1)} %constant.16.clone.join_ref) | copy-start | bytes 3932164
where the time goes:
time: 148 us
  blocking collectives  126 us (85%)
  Pallas kernels  20.7 us (14%)
    all_to_all x8, blocking collectives, exchange(): return lax.all_to_all(block, axis, split_axis=0, concat_axis=0, tiled=True)  126 us
    pallas_call x1, Pallas kernels, layer_call(): pl.pallas_call(layer_kernel, in_specs=[vmem(), anywhere(), anywhere(), an...  7.62 us
    pallas_call x1, Pallas kernels, last_call(): pl.pallas_call(last_kernel, in_specs=[vmem(), anywhere(), anywhere(), vme...  5.72 us
    pallas_call x1, Pallas kernels, first_call(): pl.pallas_call(first_kernel, in_specs=[anywhere()] * 3, out_specs=vmem(),...  4.36 us

commit v1 on v0

--- a/solution.py
+++ b/solution.py
@@ -31,10 +31,9 @@
 f32 = jnp.float32
 bf16 = jnp.bfloat16
 VMEM_LIMIT = 8 * 1024 * 1024
-WIDE_LIMIT = 16 * 1024 * 1024
-FIRST_LIMIT = 62200000
+WIDE_LIMIT = 20 * 1024 * 1024
 DEEP_ROWS = 2 * 2 * LANES
-TABLE_ROWS = DEEP_ROWS + 2 * KINDS
+TABLE_ROWS = DEEP_ROWS + NX
 
 GROUPS = (0, 160, 320, 480)
 
@@ -106,13 +105,18 @@
     return jnp.where(lane < 2 * C, turned, 0.0)
 
 
+PAIR = 2
+
+
 def wide_forward(tables, values, coef_ref, channel):
     high, low = split(values)
-    tall = dot(tables, high, ((1,), (1,)))
-    part = tall[:KINDS] + tall[KINDS:] + dot(tables[:KINDS], low, ((1,), (1,)))
-    for k, start in enumerate(GROUPS):
-        coef_ref[pl.ds(start + channel, 8, stride=C), :] = part[8 * k : 8 * k + 8]
-    coef_ref[pl.ds(EXTRA + channel, 1), :] = part[32:33]
+    wide = dot(high, tables)
+    part = wide[:, :LANES] + wide[:, LANES:] + dot(low, tables[:, :LANES])
+    for n in range(values.shape[0] // LANES):
+        rows = part[LANES * n : LANES * n + LANES].T
+        for k, start in enumerate(GROUPS):
+            coef_ref[pl.ds(start + channel + n, 8, stride=C), :] = rows[8 * k : 8 * k + 8]
+        coef_ref[pl.ds(EXTRA + channel + n, 1), :] = rows[32:33]
 
 
 def wide_inverse(coef_ref, table, channel):
@@ -216,8 +220,9 @@
     deep_copy.wait()
     for k in range(STEPS):
         copies[k].wait()
-        for channel in range(k * STEP_C, k * STEP_C + STEP_C):
-            wide_forward(deep[DEEP_ROWS:, :NX], values[channel], coef, channel)
+        for channel in range(k * STEP_C, k * STEP_C + STEP_C, PAIR):
+            both = values[channel : channel + PAIR].reshape(PAIR * LANES, NX)
+            wide_forward(deep[DEEP_ROWS:, : 2 * LANES], both, coef, channel)
     weights_copy.wait()
     pack_weights(weights, out_ref)
     deep_forward(deep, coef, out_ref)
@@ -235,26 +240,25 @@
     return pltpu.CompilerParams(vmem_limit_bytes=limit)
 
 
-def deep_scratch():
-    return pltpu.VMEM((TABLE_ROWS, 3 * LANES), bf16)
-
-
 def first_call(deep, values, weights):
     shape = (GZ, SEND_ROWS + WEIGHT_ROWS, 128)
+    operands = (deep, values, weights)
     return pl.pallas_call(
         first_kernel,
-        in_specs=[anywhere()] * 3,
-        out_specs=vmem(),
-        out_shape=jax.ShapeDtypeStruct(shape, f32),
+        in_specs=[pl.BlockSpec(memory_space=pltpu.HBM)] * len(operands),
+        out_specs=[vmem()] * 2,
+        out_shape=[
+            jax.ShapeDtypeStruct(shape, f32),
+            jax.ShapeDtypeStruct((TABLE_ROWS, 3 * LANES), bf16),
+        ],
         scratch_shapes=[
-            deep_scratch(),
             pltpu.VMEM(values.shape, f32),
             pltpu.VMEM(weights.shape, f32),
             pltpu.VMEM((COEF_ROWS, LANES), f32),
-            pltpu.SemaphoreType.DMA((STEPS + 2,)),
+            pltpu.SemaphoreType.DMA((STEPS + 3,)),
         ],
-        compiler_params=params(FIRST_LIMIT),
-    )(deep, values, weights)
+        compiler_params=params(WIDE_LIMIT),
+    )(*(pltpu.with_memory_space_constraint(a, pltpu.HBM) for a in operands))
 
 
 def join_kernel(block_ref, out_ref):
@@ -291,7 +295,7 @@
     )(block)
 
 
-def fork_blocks(block_ref, out_ref):
+def fork_blocks(block_ref, out_ref, copies):
     blocks = [block_ref[0:8, :]]
     differences = []
     for f in range(1, 16):
@@ -305,16 +309,16 @@
         row = jnp.concatenate([b[:, lane : lane + C] for b in blocks], 1)
         for t in range(TILES):
             piece = row[:, 128 * t : 128 * t + 128]
-            for g in range(GZ):
+            for g in range(copies):
                 out_ref[g, 32 * t + 8 * k : 32 * t + 8 * k + 8, :] = piece
 
 
 def fork_kernel(block_ref, out_ref):
-    fork_blocks(block_ref, out_ref)
+    fork_blocks(block_ref, out_ref, 1)
 
 
 def fork_grads_kernel(block_ref, modes_ref, grad_ref, out_ref):
-    fork_blocks(block_ref, out_ref)
+    fork_blocks(block_ref, out_ref, GZ)
     for ky in range(4):
         out_ref[:, SEND_ROWS + ky, :] = modes_ref[8 * ky : 8 * ky + 8, :]
         out_ref[:, SEND_ROWS + 4 + ky, :] = grad_ref[8 * ky : 8 * ky + 8, :]
@@ -326,7 +330,7 @@
         fork_grads_kernel if grads else fork_kernel,
         in_specs=[vmem()] * (1 + len(grads)),
         out_specs=vmem(),
-        out_shape=jax.ShapeDtypeStruct((GZ, rows, 128), f32),
+        out_shape=jax.ShapeDtypeStruct((GZ if grads else 1, rows, 128), f32),
         compiler_params=params(),
     )(block, *grads)
 
@@ -461,68 +465,53 @@
     return tall[: 8 * C] + tall[8 * C :] + dot(blocks[: 8 * C], low)
 
 
+def bypass_rows(bypass, dims, values_ref, field):
+    blocks = bypass_blocks(bypass, dims)
+    for y in range(YL):
+        for half in range(2):
+            rows = slice(8 * half, 8 * half + 8)
+            place = slice(y * ZL + 8 * half, y * ZL + 8 * half + 8)
+            values = values_ref[:, y, rows, :].reshape(8 * C, NX)
+            field[:, place, :] = bypass_product(blocks, values).reshape(C, 8, NX)
+
+
 def layer_kernel(
-    back_ref, deep_hbm, bypass_hbm, bias_hbm, block_ref, values_hbm, cot_hbm,
-    out_hbm, slope_hbm, send_ref, deep, bypass, bias, values, cots, field, coef, blocks,
-    small_sems, value_sems, cot_sems, out_sems, slope_sems
+    back_ref, deep, bypass_ref, bias_hbm, block_ref, values_ref, cot_ref, out_hbm, slope_ref,
+    send_ref, bias, field, outs, coef, coef_next, small_sems, sems
 ):
     fetch = Fetch(small_sems)
-    deep_copy = fetch_deep(fetch, deep_hbm, deep)
-    bypass_copy = fetch.start(bypass_hbm, bypass)
     bias_copy = fetch.start(bias_hbm, bias)
 
-    def value_copy(y):
-        return pltpu.make_async_copy(values_hbm.at[:, y], values.at[:, y], value_sems.at[y])
-
-    def cot_copy(y):
-        return pltpu.make_async_copy(cot_hbm.at[:, y], cots.at[:, y], cot_sems.at[y])
-
-    def out_copy(y):
-        return pltpu.make_async_copy(values.at[:, y], out_hbm.at[:, y], out_sems.at[y])
-
-    def slope_copy(y):
-        return pltpu.make_async_copy(cots.at[:, y], slope_hbm.at[:, y], slope_sems.at[y])
-
-    for y in range(YL):
-        value_copy(y).start()
-        cot_copy(y).start()
-    deep_copy.wait()
+    def out_copy(channel):
+        return pltpu.make_async_copy(outs.at[channel], out_hbm.at[channel], sems.at[channel])
+
+    bypass_rows(bypass_ref[...], ((1,), (1,)), values_ref, field)
     deep_inverse(deep, block_ref, coef)
-    bypass_copy.wait()
-    blocks[...] = bypass_blocks(bypass[...], ((1,), (1,)))
     bias_copy.wait()
-    for channel in range(C):
-        field[channel] = wide_inverse(coef, back_ref[...], channel) + bias[channel]
-
-    @pl.loop(0, YL)
-    def _(y):
-        value_copy(y).wait()
-        cot_copy(y).wait()
-        for half in range(2):
-            rows = pl.ds(8 * half, 8)
-            place = pl.ds(pl.multiple_of(y * ZL + 8 * half, 8), 8)
-            before = bypass_product(
-                blocks[...], values[:, y, rows, :].reshape(8 * C, NX)
-            ) + field[:, place, :].reshape(8 * C, NX)
+    for step in range(C // PAIR):
+        slopes = []
+        for channel in range(PAIR * step, PAIR * step + PAIR):
+            before = wide_inverse(coef, back_ref[...], channel) + field[channel] + bias[channel]
             square = before * before
             bend = jnp.tanh(before * (ROOT + (ROOT * CUBE) * square))
             half_up = 0.5 + 0.5 * bend
             rate = half_up + (half_up - half_up * half_up) * before * (
                 2.0 * ROOT + (6.0 * ROOT * CUBE) * square
             )
-            cot = cots[:, y, rows, :].reshape(8 * C, NX)
-            values[:, y, rows, :] = (before * half_up).reshape(C, 8, NX)
-            cots[:, y, rows, :] = (cot * rate).reshape(C, 8, NX)
-        out_copy(y).start()
-        slope_copy(y).start()
-
-    clear_extra(coef)
+            slope = cot_ref[channel].reshape(LANES, NX) * rate
+            outs[channel] = (before * half_up).reshape(YL, ZL, NX)
+            out_copy(channel).start()
+            slope_ref[channel] = slope.reshape(YL, ZL, NX)
+            slopes.append(slope)
+        wide_forward(deep[DEEP_ROWS:, : 2 * LANES], jnp.concatenate(slopes, 0), coef_next, PAIR * step)
+    clear_extra(coef_next)
+    deep_forward(deep, coef_next, send_ref)
     for channel in range(C):
-        wide_forward(deep[DEEP_ROWS:, :NX], cots[channel].reshape(LANES, NX), coef, channel)
-    deep_forward(deep, coef, send_ref)
-    for y in range(YL):
-        out_copy(y).wait()
-        slope_copy(y).wait()
+        out_copy(channel).wait()
+
+
+def grid_shape():
+    return jax.ShapeDtypeStruct((C, YL, ZL, NX), f32)
 
 
 def grid_buffer():
@@ -530,53 +519,37 @@
 
 
 def layer_call(back, deep, bypass, bias, block, values, cotangent):
-    grid_shape = jax.ShapeDtypeStruct((C, YL, ZL, NX), f32)
-    many = pltpu.SemaphoreType.DMA((YL,))
     return pl.pallas_call(
         layer_kernel,
-        in_specs=[vmem(), anywhere(), anywhere(), anywhere(), vmem()]
-        + [anywhere()] * 2,
-        out_specs=[anywhere(), anywhere(), vmem()],
+        in_specs=[vmem(), vmem(), vmem(), anywhere(), vmem(), vmem(), vmem()],
+        out_specs=[anywhere(), vmem(), vmem()],
         out_shape=[
-            grid_shape,
-            grid_shape,
+            grid_shape(),
+            grid_shape(),
             jax.ShapeDtypeStruct((GZ, SEND_ROWS, 128), f32),
         ],
         scratch_shapes=[
-            deep_scratch(),
-            pltpu.VMEM((C, C), f32),
             pltpu.SMEM((C,), f32),
+            pltpu.VMEM((C, LANES, NX), f32),
             grid_buffer(),
-            grid_buffer(),
-            pltpu.VMEM((C, LANES, NX), f32),
             pltpu.VMEM((COEF_ROWS, LANES), f32),
-            pltpu.VMEM((16 * C, 8 * C), bf16),
-            pltpu.SemaphoreType.DMA((3,)),
-            many,
-            many,
-            many,
-            many,
+            pltpu.VMEM((COEF_ROWS, LANES), f32),
+            pltpu.SemaphoreType.DMA((2,)),
+            pltpu.SemaphoreType.DMA((C,)),
         ],
         compiler_params=params(WIDE_LIMIT),
     )(back, deep, bypass, bias, block, values, cotangent)
 
 
 def last_kernel(
-    back_ref, deep_hbm, bypass_hbm, block_ref, slope_hbm, out_hbm, weight_hbm, deep, bypass,
-    slopes, field, coef, blocks, weight, modes_rows, grad_rows, small_sems, slope_sems, out_sems
+    back_ref, deep, bypass_ref, block_ref, slope_ref, out_hbm, weight_hbm, field, outs, coef,
+    weight, modes_rows, grad_rows, small_sems, sems
 ):
     fetch = Fetch(small_sems)
-    deep_copy = fetch_deep(fetch, deep_hbm, deep)
-    bypass_copy = fetch.start(bypass_hbm, bypass)
-
-    def slope_copy(y):
-        return pltpu.make_async_copy(slope_hbm.at[:, y], slopes.at[:, y], slope_sems.at[y])
 
     def out_copy(y):
-        return pltpu.make_async_copy(slopes.at[:, y], out_hbm.at[:, y], out_sems.at[y])
-
-    for y in range(YL):
-        slope_copy(y).start()
+        return pltpu.make_async_copy(outs.at[:, y], out_hbm.at[:, y], sems.at[y])
+
     for ky in range(4):
         for low in range(2):
             rows = pl.ds(low, GZ, stride=2)
@@ -591,25 +564,18 @@
             weight[channel, ky] = (real * grad_real + imag * grad_imag)[:, :C]
             weight[channel, 4 + ky] = (real * grad_imag - imag * grad_real)[:, :C]
     weight_copy = fetch.start(weight, weight_hbm)
-    deep_copy.wait()
     deep_inverse(deep, block_ref, coef)
-    bypass_copy.wait()
-    blocks[...] = bypass_blocks(bypass[...], ((1,), (0,)))
     for channel in range(C):
         field[channel] = wide_inverse(coef, back_ref[...], channel)
-
-    @pl.loop(0, YL)
-    def _(y):
-        slope_copy(y).wait()
+    blocks = bypass_blocks(bypass_ref[...], ((1,), (0,)))
+    for y in range(YL):
         for half in range(2):
-            rows = pl.ds(8 * half, 8)
-            place = pl.ds(pl.multiple_of(y * ZL + 8 * half, 8), 8)
-            total = bypass_product(
-                blocks[...], slopes[:, y, rows, :].reshape(8 * C, NX)
-            ) + field[:, place, :].reshape(8 * C, NX)
-            slopes[:, y, rows, :] = total.reshape(C, 8, NX)
+            rows = slice(8 * half, 8 * half + 8)
+            place = slice(y * ZL + 8 * half, y * ZL + 8 * half + 8)
+            slopes = slope_ref[:, y, rows, :].reshape(8 * C, NX)
+            total = bypass_product(blocks, slopes) + field[:, place, :].reshape(8 * C, NX)
+            outs[:, y, rows, :] = total.reshape(C, 8, NX)
         out_copy(y).start()
-
     for y in range(YL):
         out_copy(y).wait()
     weight_copy.wait()
@@ -617,28 +583,20 @@
 
 def last_call(back, deep, bypass, block, slopes):
     weight_shape = (C, 8, MODES, C)
-    many = pltpu.SemaphoreType.DMA((YL,))
     return pl.pallas_call(
         last_kernel,
-        in_specs=[vmem(), anywhere(), anywhere(), vmem(), anywhere()],
+        in_specs=[vmem()] * 5,
         out_specs=[anywhere(), anywhere()],
-        out_shape=[
-            jax.ShapeDtypeStruct((C, YL, ZL, NX), f32),
-            jax.ShapeDtypeStruct(weight_shape, f32),
-        ],
+        out_shape=[grid_shape(), jax.ShapeDtypeStruct(weight_shape, f32)],
         scratch_shapes=[
-            deep_scratch(),
-            pltpu.VMEM((C, C), f32),
+            pltpu.VMEM((C, LANES, NX), f32),
             grid_buffer(),
-            pltpu.VMEM((C, LANES, NX), f32),
             pltpu.VMEM((COEF_ROWS, LANES), f32),
-            pltpu.VMEM((16 * C, 8 * C), bf16),
             pltpu.VMEM(weight_shape, f32),
             pltpu.VMEM((MODES, 128), f32),
             pltpu.VMEM((MODES, 128), f32),
-            pltpu.SemaphoreType.DMA((3,)),
-            many,
-            many,
+            pltpu.SemaphoreType.DMA((1,)),
+            pltpu.SemaphoreType.DMA((YL,)),
         ],
         compiler_params=params(WIDE_LIMIT),
     )(back, deep, bypass, block, slopes)
@@ -658,8 +616,9 @@
     back = jnp.asarray(np.concatenate([wide_high, wide_low, wide_high, nothing], 0))
     deep_high, deep_low = halves(deep_table())
     deep = np.concatenate([deep_high, deep_low, deep_high], 3).reshape(GZ, DEEP_ROWS, 3 * LANES)
-    wide = np.concatenate([wide_high, wide_low], 0)
-    wide = np.concatenate([wide, np.zeros((2 * KINDS, LANES), ml_dtypes.bfloat16)], 1)
+    wide = np.zeros((NX, 3 * LANES), ml_dtypes.bfloat16)
+    wide[:, :KINDS] = wide_high.T
+    wide[:, LANES : LANES + KINDS] = wide_low.T
     deep = np.concatenate([deep, np.broadcast_to(wide, (GZ,) + wide.shape)], 1)
     deep = jnp.asarray(deep)
     joins = jnp.asarray(join_table().astype(ml_dtypes.bfloat16))
@@ -668,9 +627,10 @@
     weights = jnp.transpose(spectral_weights, (0, 2, 3, 4, 5, 1)).reshape(C, 8, MODES, C)
     values = grid_values.reshape(C, LANES, NX)
 
-    first = exchange(first_call(deep, values, weights), "gz")
+    sent, deep = first_call(deep, values, weights)
+    first = exchange(sent, "gz")
     rows, modes, mixing = mix_call(lat, over_y(join_call(first)), first)
-    got = exchange(fork_call(over_y(rows)), "gz")
+    got = lax.all_gather(fork_call(over_y(rows)), "gz", axis=0, tiled=True)
     output, slopes, sent = layer_call(
         back, deep, bypass_weight, bias_vector, got, grid_values, cotangent
     )

time: 148 us -> 142 us (0.959)
  Pallas kernels: 20.7 us -> 15.9 us
    all_to_all x8 -> x7, blocking collectives: 126 us -> 108 us  [exchange(): return lax.all_to_all(block, axis, split_axis=0, concat_axis=0, tiled=True)]
    all_gather x0 -> x1, blocking collectives: none -> 16.5 us  [shards(): got = lax.all_gather(fork_call(over_y(rows)), 'gz', axis=0, tiled=True)]
    pallas_call x3, Pallas kernels: 17.7 us -> 13 us  [the longest x1 5.89 us: layer_call(): pl.pallas_call(layer_kernel, in_specs=[vmem(), vmem(), vmem(), anywhere()...]
where the time goes in v1:
time: 142 us
  blocking collectives  125 us (88%)
  Pallas kernels  15.9 us (11%)
    all_to_all x7, blocking collectives, exchange(): return lax.all_to_all(block, axis, split_axis=0, concat_axis=0, tiled=True)  108 us
    all_gather x1, blocking collectives, shards(): got = lax.all_gather(fork_call(over_y(rows)), 'gz', axis=0, tiled=True)  16.5 us
    pallas_call x1, Pallas kernels, layer_call(): pl.pallas_call(layer_kernel, in_specs=[vmem(), vmem(), vmem(), anywhere()...  5.89 us
    pallas_call x1, Pallas kernels, last_call(): pl.pallas_call(last_kernel, in_specs=[vmem()] * 5, out_specs=[anywhere(),...  3.6 us
    pallas_call x1, Pallas kernels, first_call(): pl.pallas_call(first_kernel, in_specs=[pl.BlockSpec(memory_space=pltpu.HB...  3.49 us

profile of v1, /device:TPU:1, one launch (start us, length us, event | category | flops | bytes accessed | tf_op | source)
XLA Modules:
  0.0 141.6 jit_solution(14136811878507566976)
XLA Ops:
  0.6 0.0 copy-start.7
  0.6 3.5 %shard_map.139 = (f32[8,216,128]{2,1,0:T(8,128)S(1)}, bf16[768,384]{1,0:T(8,128)(2,1)S(1)}) custom-call(bf16[8,768,384]{2,1,0:T(8,128)(2,1)} %constant.15.clone.deep_hbm, f32[20,128,256]{2,1,0:T(8,128)} %bitcast.17, f32[20,8,16,20]{3,2,1,0:T(8,128)} %bitcast.26), custom_call_target="tpu_custom_call" | custom-call | tf_op jit(solution)/shard_map/pallas_call | solution.py:246
  4.1 0.0 copy-start.4
  4.2 0.0 copy-start.5
  4.2 0.0 copy-start.6
  4.2 0.0 copy-start
  4.2 0.0 copy-start.1
  4.2 0.0 copy-start.3
  4.2 0.0 copy-start.8
  4.2 0.0 copy-start.9
  4.2 19.5 %all_to_all.35.block_ref.first_ref = f32[8,216,128]{2,1,0:T(8,128)S(1)} all-to-all(f32[8,216,128]{2,1,0:T(8,128)S(1)} %get-tuple-element.16), channel_id=1, replica_groups=mesh['gy'=32,'gz'=8] {'gz'}, dimensions={0} | all-to-all | bytes 1769472 | tf_op jit(solution)/shard_map/all_to_all | solution.py:606
  23.7 0.2 shard_map.140
  24.0 20.0 %all_to_all.36 = f32[32,8,128]{2,1,0:T(8,128)S(1)} all-to-all(f32[32,8,128]{2,1,0:T(8,128)S(1)} %bitcast.22), channel_id=1, replica_groups=mesh['gy'=32,'gz'=8] {'gy'}, dimensions={0} | all-to-all | bytes 262144 | tf_op jit(solution)/shard_map/all_to_all | solution.py:606
  44.0 0.0 copy-done.7
  44.0 0.0 copy-done.4
  44.0 0.0 copy-done.5
  44.0 0.0 copy-done.6
  44.0 1.2 shard_map.141
  45.2 12.7 %all_to_all.37 = f32[32,8,128]{2,1,0:T(8,128)S(1)} all-to-all(f32[32,8,128]{2,1,0:T(8,128)S(1)} %bitcast.25), channel_id=1, replica_groups=mesh['gy'=32,'gz'=8] {'gy'}, dimensions={0} | all-to-all | bytes 262144 | tf_op jit(solution)/shard_map/all_to_all | solution.py:606
  57.9 0.2 shard_map.142
  58.1 16.5 %all_gather.3.block_ref = f32[8,160,128]{2,1,0:T(8,128)S(1)} all-gather(f32[1,160,128]{2,1,0:T(8,128)S(1)} %shard_map.142), channel_id=1, replica_groups=mesh['gy'=32,'gz'=8] {'gz'}, dimensions={0}, use_global_device_ids=true | all-gather | bytes 737280 | tf_op jit(solution)/shard_map/all_gather | solution.py:633
  74.7 0.0 copy-done
  74.7 0.0 copy-done.1
  74.7 0.0 copy-done.3
  74.7 0.0 copy-done.8
  74.7 0.0 copy-done.9
  74.7 5.9 %shard_map.143 = (f32[20,8,16,256]{3,2,1,0:T(8,128)}, f32[20,8,16,256]{3,2,1,0:T(8,128)S(1)}, f32[8,160,128]{2,1,0:T(8,128)S(1)}) custom-call(bf16[128,256]{1,0:T(8,128)(2,1)S(1)} %copy-done.3, bf16[768,384]{1,0:T(8,128)(2,1)S(1)} %get-tuple-element.15.deep, f32[20,20]{1,0:T(8,128)S(1)} %copy-done.8, f32[20]{0:T(128)S(1)} %copy-done.9, ...), custom_call_target="tpu_custom_call" | custom-call | tf_op jit(solution)/shard_map/pallas_call | solution.py:522
  80.6 0.0 copy-start.2
  80.6 13.8 %all_to_all.38.block_ref = f32[8,160,128]{2,1,0:T(8,128)S(1)} all-to-all(f32[8,160,128]{2,1,0:T(8,128)S(1)} %get-tuple-element.19), channel_id=1, replica_groups=mesh['gy'=32,'gz'=8] {'gz'}, dimensions={0} | all-to-all | bytes 1310720 | tf_op jit(solution)/shard_map/all_to_all | solution.py:606
  94.4 0.2 shard_map.144
  94.6 12.4 %all_to_all.39 = f32[32,8,128]{2,1,0:T(8,128)S(1)} all-to-all(f32[32,8,128]{2,1,0:T(8,128)S(1)} %bitcast.21), channel_id=1, replica_groups=mesh['gy'=32,'gz'=8] {'gy'}, dimensions={0} | all-to-all | bytes 262144 | tf_op jit(solution)/shard_map/all_to_all | solution.py:606
  106.9 0.0 copy-done.2
  107.0 0.9 shard_map.145
  107.9 12.7 %all_to_all.40 = f32[32,8,128]{2,1,0:T(8,128)S(1)} all-to-all(f32[32,8,128]{2,1,0:T(8,128)S(1)} %bitcast.24), channel_id=1, replica_groups=mesh['gy'=32,'gz'=8] {'gy'}, dimensions={0} | all-to-all | bytes 262144 | tf_op jit(solution)/shard_map/all_to_all | solution.py:606
  120.6 0.2 shard_map.146
  120.8 17.2 %all_to_all.41.block_ref = f32[8,168,128]{2,1,0:T(8,128)S(1)} all-to-all(f32[8,168,128]{2,1,0:T(8,128)S(1)} %shard_map.146), channel_id=1, replica_groups=mesh['gy'=32,'gz'=8] {'gz'}, dimensions={0} | all-to-all | bytes 1376256 | tf_op jit(solution)/shard_map/all_to_all | solution.py:606
  137.9 3.6 %shard_map.147 = (f32[20,8,16,256]{3,2,1,0:T(8,128)}, f32[20,8,16,20]{3,2,1,0:T(8,128)}) custom-call(bf16[128,256]{1,0:T(8,128)(2,1)S(1)} %copy-done.3, bf16[768,384]{1,0:T(8,128)(2,1)S(1)} %get-tuple-element.15.deep, f32[20,20]{1,0:T(8,128)S(1)} %copy-done.8, f32[8,168,128]{2,1,0:T(8,128)S(1)} %all_to_all.41.block_ref, ...), custom_call_target="tpu_custom_call" | custom-call | tf_op jit(solution)/shard_map/pallas_call | solution.py:586
Async XLA Ops:
  0.6 43.3 %copy-start.7 = (bf16[64,256]{1,0:T(8,128)(2,1)S(1)}, bf16[64,256]{1,0:T(8,128)(2,1)}, u32[]{:S(2)}) copy-start(bf16[64,256]{1,0:T(8,128)(2,1)} %constant.17.clone.lat_h) | copy-start | bytes 98308
  4.1 39.8 %copy-start.4 = (bf16[256,64]{1,0:T(8,128)(2,1)S(1)}, bf16[256,64]{1,0:T(8,128)(2,1)}, u32[]{:S(2)}) copy-start(bf16[256,64]{1,0:T(8,128)(2,1)} %constant.20.clone.back_l) | copy-start | bytes 98308
  4.2 39.8 %copy-start.5 = (bf16[256,64]{1,0:T(8,128)(2,1)S(1)}, bf16[256,64]{1,0:T(8,128)(2,1)}, u32[]{:S(2)}) copy-start(bf16[256,64]{1,0:T(8,128)(2,1)} %constant.19.clone.back_h) | copy-start | bytes 98308
  4.2 39.8 %copy-start.6 = (bf16[64,256]{1,0:T(8,128)(2,1)S(1)}, bf16[64,256]{1,0:T(8,128)(2,1)}, u32[]{:S(2)}) copy-start(bf16[64,256]{1,0:T(8,128)(2,1)} %constant.18.clone.lat_l) | copy-start | bytes 98308
  4.2 70.5 %copy-start = (f32[20,8,16,256]{3,2,1,0:T(8,128)S(1)}, f32[20,8,16,256]{3,2,1,0:T(8,128)}, u32[]{:S(2)}) copy-start(f32[20,8,16,256]{3,2,1,0:T(8,128)} %values_ref.1) | copy-start | bytes 7864324
  4.2 70.5 %copy-start.1 = (f32[20,8,16,256]{3,2,1,0:T(8,128)S(1)}, f32[20,8,16,256]{3,2,1,0:T(8,128)}, u32[]{:S(2)}) copy-start(f32[20,8,16,256]{3,2,1,0:T(8,128)} %cot_ref.1) | copy-start | bytes 7864324
  4.2 70.5 %copy-start.3 = (bf16[128,256]{1,0:T(8,128)(2,1)S(1)}, bf16[128,256]{1,0:T(8,128)(2,1)}, u32[]{:S(2)}) copy-start(bf16[128,256]{1,0:T(8,128)(2,1)} %constant.14.clone.back_ref) | copy-start | bytes 196612
  4.2 70.5 %copy-start.8 = (f32[20,20]{1,0:T(8,128)S(1)}, f32[20,20]{1,0:T(8,128)}, u32[]{:S(2)}) copy-start(f32[20,20]{1,0:T(8,128)} %bypass_ref.3) | copy-start | bytes 4804
  4.2 70.5 %copy-start.9 = (f32[20]{0:T(128)S(1)}, f32[20]{0:T(128)}, u32[]{:S(2)}) copy-start(f32[20]{0:T(128)} %bias_hbm.1) | copy-start | bytes 244
  80.6 26.4 %copy-start.2 = (bf16[5120,128]{1,0:T(8,128)(2,1)S(1)}, bf16[5120,128]{1,0:T(8,128)(2,1)}, u32[]{:S(2)}) copy-start(bf16[5120,128]{1,0:T(8,128)(2,1)} %constant.16.clone.join_ref) | copy-start | bytes 3932164

commit v2 on v1

--- a/solution.py
+++ b/solution.py
@@ -23,7 +23,7 @@
 TILES = 5
 SEND_ROWS = TILES * 32
 WEIGHT_ROWS = 56
-GRAD_ROWS = 8
+GRAD_ROWS = 64
 EXTRA = 748
 COEF_ROWS = 768
 KINDS = 40
@@ -33,7 +33,6 @@
 VMEM_LIMIT = 8 * 1024 * 1024
 WIDE_LIMIT = 20 * 1024 * 1024
 DEEP_ROWS = 2 * 2 * LANES
-TABLE_ROWS = DEEP_ROWS + NX
 
 GROUPS = (0, 160, 320, 480)
 
@@ -109,11 +108,10 @@
 
 
 def wide_forward(tables, values, coef_ref, channel):
-    high, low = split(values)
-    wide = dot(high, tables)
-    part = wide[:, :LANES] + wide[:, LANES:] + dot(low, tables[:, :LANES])
+    part = dot(jnp.concatenate(split(values), 1), tables)
     for n in range(values.shape[0] // LANES):
         rows = part[LANES * n : LANES * n + LANES].T
+        rows = rows[:KINDS] + rows[64 : 64 + KINDS]
         for k, start in enumerate(GROUPS):
             coef_ref[pl.ds(start + channel + n, 8, stride=C), :] = rows[8 * k : 8 * k + 8]
         coef_ref[pl.ds(EXTRA + channel + n, 1), :] = rows[32:33]
@@ -172,7 +170,9 @@
     coef_ref[320:640, :] = product(1, rows[320:])
 
 
-STEP_C = 4
+STEP_C = 10
+OUT_C = 2
+OUT_Y = 1
 STEPS = C // STEP_C
 
 
@@ -207,24 +207,27 @@
 
 
 def first_kernel(
-    deep_hbm, values_hbm, weights_hbm, out_ref, deep, values, weights, coef, sems
+    deep_hbm, tables_hbm, values_hbm, weights_hbm, out_ref, deep, tables, values, weights, coef,
+    sems
 ):
     fetch = Fetch(sems)
-    deep_copy = fetch_deep(fetch, deep_hbm, deep)
+    tables_copy = fetch.start(tables_hbm, tables)
     copies = []
     for k in range(STEPS):
         part = pl.ds(k * STEP_C, STEP_C)
         copies.append(fetch.start(values_hbm.at[part], values.at[part]))
+    deep_copy = fetch_deep(fetch, deep_hbm, deep)
     weights_copy = fetch.start(weights_hbm, weights)
     clear_extra(coef)
-    deep_copy.wait()
+    tables_copy.wait()
     for k in range(STEPS):
         copies[k].wait()
         for channel in range(k * STEP_C, k * STEP_C + STEP_C, PAIR):
             both = values[channel : channel + PAIR].reshape(PAIR * LANES, NX)
-            wide_forward(deep[DEEP_ROWS:, : 2 * LANES], both, coef, channel)
+            wide_forward(tables[...], both, coef, channel)
     weights_copy.wait()
     pack_weights(weights, out_ref)
+    deep_copy.wait()
     deep_forward(deep, coef, out_ref)
 
 
@@ -240,16 +243,17 @@
     return pltpu.CompilerParams(vmem_limit_bytes=limit)
 
 
-def first_call(deep, values, weights):
+def first_call(deep, tables, values, weights):
     shape = (GZ, SEND_ROWS + WEIGHT_ROWS, 128)
-    operands = (deep, values, weights)
+    operands = (deep, tables, values, weights)
     return pl.pallas_call(
         first_kernel,
         in_specs=[pl.BlockSpec(memory_space=pltpu.HBM)] * len(operands),
-        out_specs=[vmem()] * 2,
+        out_specs=[vmem()] * 3,
         out_shape=[
             jax.ShapeDtypeStruct(shape, f32),
-            jax.ShapeDtypeStruct((TABLE_ROWS, 3 * LANES), bf16),
+            jax.ShapeDtypeStruct(deep.shape[1:], bf16),
+            jax.ShapeDtypeStruct(tables.shape, bf16),
         ],
         scratch_shapes=[
             pltpu.VMEM(values.shape, f32),
@@ -295,7 +299,7 @@
     )(block)
 
 
-def fork_blocks(block_ref, out_ref, copies):
+def fork_blocks(block_ref, out_ref):
     blocks = [block_ref[0:8, :]]
     differences = []
     for f in range(1, 16):
@@ -308,20 +312,17 @@
         lane = 64 * (k // 2) + C * (k % 2)
         row = jnp.concatenate([b[:, lane : lane + C] for b in blocks], 1)
         for t in range(TILES):
-            piece = row[:, 128 * t : 128 * t + 128]
-            for g in range(copies):
-                out_ref[g, 32 * t + 8 * k : 32 * t + 8 * k + 8, :] = piece
+            out_ref[0, 32 * t + 8 * k : 32 * t + 8 * k + 8, :] = row[:, 128 * t : 128 * t + 128]
 
 
 def fork_kernel(block_ref, out_ref):
-    fork_blocks(block_ref, out_ref, 1)
+    fork_blocks(block_ref, out_ref)
 
 
 def fork_grads_kernel(block_ref, modes_ref, grad_ref, out_ref):
-    fork_blocks(block_ref, out_ref, GZ)
-    for ky in range(4):
-        out_ref[:, SEND_ROWS + ky, :] = modes_ref[8 * ky : 8 * ky + 8, :]
-        out_ref[:, SEND_ROWS + 4 + ky, :] = grad_ref[8 * ky : 8 * ky + 8, :]
+    fork_blocks(block_ref, out_ref)
+    out_ref[0, SEND_ROWS : SEND_ROWS + 32, :] = modes_ref[...]
+    out_ref[0, SEND_ROWS + 32 :, :] = grad_ref[...]
 
 
 def fork_call(block, *grads):
@@ -330,7 +331,7 @@
         fork_grads_kernel if grads else fork_kernel,
         in_specs=[vmem()] * (1 + len(grads)),
         out_specs=vmem(),
-        out_shape=jax.ShapeDtypeStruct((GZ if grads else 1, rows, 128), f32),
+        out_shape=jax.ShapeDtypeStruct((1, rows, 128), f32),
         compiler_params=params(),
     )(block, *grads)
 
@@ -338,12 +339,15 @@
 def unpack(block_ref, c):
     left = lane_index((GZ, 128)) < 64
     rows = []
+    loaded = {}
     for ky in range(4):
         sides = []
         for low in range(2):
             unit = (c * 4 + ky) * 2 + low
-            side = block_ref[:, SEND_ROWS + unit // 3, :]
-            sides.append(turn(side, 64 * low - 40 * (unit % 3)))
+            row = SEND_ROWS + unit // 3
+            if row not in loaded:
+                loaded[row] = block_ref[:, row, :]
+            sides.append(turn(loaded[row], 64 * low - 40 * (unit % 3)))
         rows.append(jnp.where(left, sides[0], sides[1]))
     return jnp.concatenate(rows, 0)
 
@@ -456,13 +460,12 @@
     for half in split(bypass):
         wide = dot(dot(select, half, dims).astype(bf16), select, ((1,), (1,)))
         blocks.append(jnp.where(same, wide, 0.0))
-    return jnp.concatenate(blocks, 0).astype(bf16)
+    return jnp.concatenate([blocks[0], blocks[1], blocks[0]], 1).astype(bf16)
 
 
 def bypass_product(blocks, values):
     high, low = split(values)
-    tall = dot(blocks, high)
-    return tall[: 8 * C] + tall[8 * C :] + dot(blocks[: 8 * C], low)
+    return dot(blocks, jnp.concatenate([high, high, low], 0))
 
 
 def bypass_rows(bypass, dims, values_ref, field):
@@ -476,14 +479,15 @@
 
 
 def layer_kernel(
-    back_ref, deep, bypass_ref, bias_hbm, block_ref, values_ref, cot_ref, out_hbm, slope_ref,
+    back_ref, deep, tables_ref, bypass_ref, bias_hbm, block_ref, values_ref, cot_ref, out_hbm, slope_ref,
     send_ref, bias, field, outs, coef, coef_next, small_sems, sems
 ):
     fetch = Fetch(small_sems)
     bias_copy = fetch.start(bias_hbm, bias)
 
-    def out_copy(channel):
-        return pltpu.make_async_copy(outs.at[channel], out_hbm.at[channel], sems.at[channel])
+    def out_copy(part):
+        group = pl.ds(part * OUT_C, OUT_C)
+        return pltpu.make_async_copy(outs.at[group], out_hbm.at[group], sems.at[part])
 
     bypass_rows(bypass_ref[...], ((1,), (1,)), values_ref, field)
     deep_inverse(deep, block_ref, coef)
@@ -500,14 +504,15 @@
             )
             slope = cot_ref[channel].reshape(LANES, NX) * rate
             outs[channel] = (before * half_up).reshape(YL, ZL, NX)
-            out_copy(channel).start()
+            if channel % OUT_C == OUT_C - 1:
+                out_copy(channel // OUT_C).start()
             slope_ref[channel] = slope.reshape(YL, ZL, NX)
             slopes.append(slope)
-        wide_forward(deep[DEEP_ROWS:, : 2 * LANES], jnp.concatenate(slopes, 0), coef_next, PAIR * step)
+        wide_forward(tables_ref[...], jnp.concatenate(slopes, 0), coef_next, PAIR * step)
     clear_extra(coef_next)
     deep_forward(deep, coef_next, send_ref)
-    for channel in range(C):
-        out_copy(channel).wait()
+    for part in range(C // OUT_C):
+        out_copy(part).wait()
 
 
 def grid_shape():
@@ -518,10 +523,10 @@
     return pltpu.VMEM((C, YL, ZL, NX), f32)
 
 
-def layer_call(back, deep, bypass, bias, block, values, cotangent):
+def layer_call(back, deep, tables, bypass, bias, block, values, cotangent):
     return pl.pallas_call(
         layer_kernel,
-        in_specs=[vmem(), vmem(), vmem(), anywhere(), vmem(), vmem(), vmem()],
+        in_specs=[vmem()] * 4 + [anywhere()] + [vmem()] * 3,
         out_specs=[anywhere(), vmem(), vmem()],
         out_shape=[
             grid_shape(),
@@ -535,10 +540,10 @@
             pltpu.VMEM((COEF_ROWS, LANES), f32),
             pltpu.VMEM((COEF_ROWS, LANES), f32),
             pltpu.SemaphoreType.DMA((2,)),
-            pltpu.SemaphoreType.DMA((C,)),
+            pltpu.SemaphoreType.DMA((C // OUT_C,)),
         ],
         compiler_params=params(WIDE_LIMIT),
-    )(back, deep, bypass, bias, block, values, cotangent)
+    )(back, deep, tables, bypass, bias, block, values, cotangent)
 
 
 def last_kernel(
@@ -547,14 +552,17 @@
 ):
     fetch = Fetch(small_sems)
 
-    def out_copy(y):
-        return pltpu.make_async_copy(outs.at[:, y], out_hbm.at[:, y], sems.at[y])
+    def out_copy(part):
+        rows = pl.ds(part * OUT_Y, OUT_Y)
+        return pltpu.make_async_copy(outs.at[:, rows], out_hbm.at[:, rows], sems.at[part])
 
     for ky in range(4):
         for low in range(2):
             rows = pl.ds(low, GZ, stride=2)
-            modes_rows[rows, :] = turn(block_ref[:, SEND_ROWS + ky, :], 64 * low)
-            grad_rows[rows, :] = turn(block_ref[:, SEND_ROWS + 4 + ky, :], 64 * low)
+            own = SEND_ROWS + 8 * ky + lax.axis_index("gz")
+            modes_rows[rows, :] = turn(block_ref[:, pl.ds(own, 1), :].reshape(GZ, 128), 64 * low)
+            own = own + 32
+            grad_rows[rows, :] = turn(block_ref[:, pl.ds(own, 1), :].reshape(GZ, 128), 64 * low)
         modes = modes_rows[...]
         grad_real = grad_rows[...]
         grad_imag = turn(grad_real, -C)
@@ -575,9 +583,10 @@
             slopes = slope_ref[:, y, rows, :].reshape(8 * C, NX)
             total = bypass_product(blocks, slopes) + field[:, place, :].reshape(8 * C, NX)
             outs[:, y, rows, :] = total.reshape(C, 8, NX)
-        out_copy(y).start()
-    for y in range(YL):
-        out_copy(y).wait()
+        if y % OUT_Y == OUT_Y - 1:
+            out_copy(y // OUT_Y).start()
+    for part in range(YL // OUT_Y):
+        out_copy(part).wait()
     weight_copy.wait()
 
 
@@ -596,7 +605,7 @@
             pltpu.VMEM((MODES, 128), f32),
             pltpu.VMEM((MODES, 128), f32),
             pltpu.SemaphoreType.DMA((1,)),
-            pltpu.SemaphoreType.DMA((YL,)),
+            pltpu.SemaphoreType.DMA((YL // OUT_Y,)),
         ],
         compiler_params=params(WIDE_LIMIT),
     )(back, deep, bypass, block, slopes)
@@ -604,6 +613,10 @@
 
 def exchange(block, axis):
     return lax.all_to_all(block, axis, split_axis=0, concat_axis=0, tiled=True)
+
+
+def gather(block):
+    return lax.all_gather(block, "gz", axis=0, tiled=True)
 
 
 def over_y(rows):
@@ -616,28 +629,29 @@
     back = jnp.asarray(np.concatenate([wide_high, wide_low, wide_high, nothing], 0))
     deep_high, deep_low = halves(deep_table())
     deep = np.concatenate([deep_high, deep_low, deep_high], 3).reshape(GZ, DEEP_ROWS, 3 * LANES)
-    wide = np.zeros((NX, 3 * LANES), ml_dtypes.bfloat16)
-    wide[:, :KINDS] = wide_high.T
-    wide[:, LANES : LANES + KINDS] = wide_low.T
-    deep = np.concatenate([deep, np.broadcast_to(wide, (GZ,) + wide.shape)], 1)
+    tables = np.zeros((2 * NX, LANES), ml_dtypes.bfloat16)
+    tables[:NX, :KINDS] = wide_high.T
+    tables[:NX, 64 : 64 + KINDS] = wide_low.T
+    tables[NX:, :KINDS] = wide_high.T
     deep = jnp.asarray(deep)
+    tables = jnp.asarray(tables)
     joins = jnp.asarray(join_table().astype(ml_dtypes.bfloat16))
     lat_full = lat_table()
     lat = tuple(jnp.asarray(t) for t in halves(lat_full) + halves(lat_full.T.copy()))
     weights = jnp.transpose(spectral_weights, (0, 2, 3, 4, 5, 1)).reshape(C, 8, MODES, C)
     values = grid_values.reshape(C, LANES, NX)
 
-    sent, deep = first_call(deep, values, weights)
+    sent, deep, tables = first_call(deep, tables, values, weights)
     first = exchange(sent, "gz")
     rows, modes, mixing = mix_call(lat, over_y(join_call(first)), first)
-    got = lax.all_gather(fork_call(over_y(rows)), "gz", axis=0, tiled=True)
+    got = gather(fork_call(over_y(rows)))
     output, slopes, sent = layer_call(
-        back, deep, bypass_weight, bias_vector, got, grid_values, cotangent
+        back, deep, tables, bypass_weight, bias_vector, got, grid_values, cotangent
     )
 
     got = exchange(sent, "gz")
     rows, grad = adjoint_call(lat, joins, over_y(join_call(got)), mixing)
-    got = exchange(fork_call(over_y(rows), modes, grad), "gz")
+    got = gather(fork_call(over_y(rows), modes, grad))
     grad_values, weight_grad = last_call(back, deep, bypass_weight, got, slopes)
     weight_grad = weight_grad.reshape(C, 2, 1, 4, MODES, C)
     return output, grad_values, jnp.transpose(weight_grad, (0, 5, 1, 2, 3, 4))

time: 142 us -> 141 us (level)
    all_gather x1 -> x2, blocking collectives: 16.5 us -> 33.7 us  [gather(): return lax.all_gather(block, 'gz', axis=0, tiled=True)]
    all_to_all x7 -> x6, blocking collectives: 108 us -> 91.1 us  [exchange(): return lax.all_to_all(block, axis, split_axis=0, concat_axis=0, tiled=True)]
where the time goes in v2:
time: 141 us
  blocking collectives  125 us (89%)
  Pallas kernels  15.3 us (11%)
    all_to_all x6, blocking collectives, exchange(): return lax.all_to_all(block, axis, split_axis=0, concat_axis=0, tiled=True)  91.1 us
    all_gather x2, blocking collectives, gather(): return lax.all_gather(block, 'gz', axis=0, tiled=True)  33.7 us
    pallas_call x1, Pallas kernels, layer_call(): pl.pallas_call(layer_kernel, in_specs=[vmem()] * 4 + [anywhere()] + [vmem...  5.47 us
    pallas_call x1, Pallas kernels, last_call(): pl.pallas_call(last_kernel, in_specs=[vmem()] * 5, out_specs=[anywhere(),...  3.5 us
    pallas_call x1, Pallas kernels, first_call(): pl.pallas_call(first_kernel, in_specs=[pl.BlockSpec(memory_space=pltpu.HB...  3.42 us

profile of v2, /device:TPU:1, one launch (start us, length us, event | category | flops | bytes accessed | tf_op | source)
XLA Modules:
  0.0 141.1 jit_solution(11617520103171018860)
XLA Ops:
  0.6 0.0 copy-start.7
  0.6 3.4 %shard_map.148 = (f32[8,216,128]{2,1,0:T(8,128)S(1)}, bf16[512,384]{1,0:T(8,128)(2,1)S(1)}, bf16[512,128]{1,0:T(8,128)(2,1)S(1)}) custom-call(bf16[8,512,384]{2,1,0:T(8,128)(2,1)} %constant.17.clone.deep_hbm, bf16[512,128]{1,0:T(8,128)(2,1)} %constant.18.clone.tables_hbm, f32[20,128,256]{2,1,0:T(8,128)} %bitcast.17, f32[20,8,16,20]{3,2,1,0:T(8,128)} %bitcast.26), custom_call_target="tpu_custom_call" | custom-call | tf_op jit(solution)/shard_map/pallas_call | solution.py:249
  4.1 0.0 copy-start.4
  4.1 0.0 copy-start.5
  4.1 0.0 copy-start.6
  4.1 0.0 copy-start
  4.1 0.0 copy-start.1
  4.1 0.0 copy-start.3
  4.1 0.0 copy-start.8
  4.2 0.0 copy-start.9
  4.2 19.5 %all_to_all.30.block_ref.first_ref = f32[8,216,128]{2,1,0:T(8,128)S(1)} all-to-all(f32[8,216,128]{2,1,0:T(8,128)S(1)} %get-tuple-element.18), channel_id=1, replica_groups=mesh['gy'=32,'gz'=8] {'gz'}, dimensions={0} | all-to-all | bytes 1769472 | tf_op jit(solution)/shard_map/all_to_all | solution.py:615
  23.7 0.2 shard_map.149
  23.9 20.0 %all_to_all.31 = f32[32,8,128]{2,1,0:T(8,128)S(1)} all-to-all(f32[32,8,128]{2,1,0:T(8,128)S(1)} %bitcast.22), channel_id=1, replica_groups=mesh['gy'=32,'gz'=8] {'gy'}, dimensions={0} | all-to-all | bytes 262144 | tf_op jit(solution)/shard_map/all_to_all | solution.py:615
  43.9 0.0 copy-done.7
  43.9 0.0 copy-done.4
  43.9 0.0 copy-done.5
  43.9 0.0 copy-done.6
  43.9 1.2 shard_map.150
  45.1 12.7 %all_to_all.32 = f32[32,8,128]{2,1,0:T(8,128)S(1)} all-to-all(f32[32,8,128]{2,1,0:T(8,128)S(1)} %bitcast.25), channel_id=1, replica_groups=mesh['gy'=32,'gz'=8] {'gy'}, dimensions={0} | all-to-all | bytes 262144 | tf_op jit(solution)/shard_map/all_to_all | solution.py:615
  57.9 0.2 shard_map.151
  58.1 16.5 %all_gather.6.block_ref = f32[8,160,128]{2,1,0:T(8,128)S(1)} all-gather(f32[1,160,128]{2,1,0:T(8,128)S(1)} %shard_map.151), channel_id=1, replica_groups=mesh['gy'=32,'gz'=8] {'gz'}, dimensions={0}, use_global_device_ids=true | all-gather | bytes 737280 | tf_op jit(solution)/shard_map/all_gather | solution.py:619
  74.6 0.0 copy-done
  74.6 0.0 copy-done.1
  74.6 0.0 copy-done.3
  74.6 0.0 copy-done.8
  74.6 0.0 copy-done.9
  74.6 5.5 %shard_map.152 = (f32[20,8,16,256]{3,2,1,0:T(8,128)}, f32[20,8,16,256]{3,2,1,0:T(8,128)S(1)}, f32[8,160,128]{2,1,0:T(8,128)S(1)}) custom-call(bf16[128,256]{1,0:T(8,128)(2,1)S(1)} %copy-done.3, bf16[512,384]{1,0:T(8,128)(2,1)S(1)} %get-tuple-element.16.deep, bf16[512,128]{1,0:T(8,128)(2,1)S(1)} %get-tuple-element.17.tables_ref, f32[20,20]{1,0:T(8,128)S(1)} %copy-done.8, ...), custom_call_target="tpu_custom_call" | custom-call | tf_op jit(solution)/shard_map/pallas_call | solution.py:527
  80.1 0.0 copy-start.2
  80.1 13.8 %all_to_all.33.block_ref = f32[8,160,128]{2,1,0:T(8,128)S(1)} all-to-all(f32[8,160,128]{2,1,0:T(8,128)S(1)} %get-tuple-element.21), channel_id=1, replica_groups=mesh['gy'=32,'gz'=8] {'gz'}, dimensions={0} | all-to-all | bytes 1310720 | tf_op jit(solution)/shard_map/all_to_all | solution.py:615
  93.9 0.2 shard_map.153
  94.1 12.4 %all_to_all.34 = f32[32,8,128]{2,1,0:T(8,128)S(1)} all-to-all(f32[32,8,128]{2,1,0:T(8,128)S(1)} %bitcast.21), channel_id=1, replica_groups=mesh['gy'=32,'gz'=8] {'gy'}, dimensions={0} | all-to-all | bytes 262144 | tf_op jit(solution)/shard_map/all_to_all | solution.py:615
  106.5 0.0 copy-done.2
  106.5 0.9 shard_map.154
  107.4 12.7 %all_to_all.35 = f32[32,8,128]{2,1,0:T(8,128)S(1)} all-to-all(f32[32,8,128]{2,1,0:T(8,128)S(1)} %bitcast.24), channel_id=1, replica_groups=mesh['gy'=32,'gz'=8] {'gy'}, dimensions={0} | all-to-all | bytes 262144 | tf_op jit(solution)/shard_map/all_to_all | solution.py:615
  120.1 0.2 shard_map.155
  120.3 17.2 %all_gather.7.block_ref = f32[8,224,128]{2,1,0:T(8,128)S(1)} all-gather(f32[1,224,128]{2,1,0:T(8,128)S(1)} %shard_map.155), channel_id=1, replica_groups=mesh['gy'=32,'gz'=8] {'gz'}, dimensions={0}, use_global_device_ids=true | all-gather | bytes 1032192 | tf_op jit(solution)/shard_map/all_gather | solution.py:619
  137.5 3.5 %shard_map.156 = (f32[20,8,16,256]{3,2,1,0:T(8,128)}, f32[20,8,16,20]{3,2,1,0:T(8,128)}) custom-call(bf16[128,256]{1,0:T(8,128)(2,1)S(1)} %copy-done.3, bf16[512,384]{1,0:T(8,128)(2,1)S(1)} %get-tuple-element.16.deep, f32[20,20]{1,0:T(8,128)S(1)} %copy-done.8, f32[8,224,128]{2,1,0:T(8,128)S(1)} %all_gather.7.block_ref, ...), custom_call_target="tpu_custom_call" | custom-call | tf_op jit(solution)/shard_map/pallas_call | solution.py:595
Async XLA Ops:
  0.6 43.3 %copy-start.7 = (bf16[64,256]{1,0:T(8,128)(2,1)S(1)}, bf16[64,256]{1,0:T(8,128)(2,1)}, u32[]{:S(2)}) copy-start(bf16[64,256]{1,0:T(8,128)(2,1)} %constant.20.clone.lat_h) | copy-start | bytes 98308
  4.1 39.8 %copy-start.4 = (bf16[256,64]{1,0:T(8,128)(2,1)S(1)}, bf16[256,64]{1,0:T(8,128)(2,1)}, u32[]{:S(2)}) copy-start(bf16[256,64]{1,0:T(8,128)(2,1)} %constant.23.clone.back_l) | copy-start | bytes 98308
  4.1 39.8 %copy-start.5 = (bf16[256,64]{1,0:T(8,128)(2,1)S(1)}, bf16[256,64]{1,0:T(8,128)(2,1)}, u32[]{:S(2)}) copy-start(bf16[256,64]{1,0:T(8,128)(2,1)} %constant.22.clone.back_h) | copy-start | bytes 98308
  4.1 39.8 %copy-start.6 = (bf16[64,256]{1,0:T(8,128)(2,1)S(1)}, bf16[64,256]{1,0:T(8,128)(2,1)}, u32[]{:S(2)}) copy-start(bf16[64,256]{1,0:T(8,128)(2,1)} %constant.21.clone.lat_l) | copy-start | bytes 98308
  4.1 70.5 %copy-start = (f32[20,8,16,256]{3,2,1,0:T(8,128)S(1)}, f32[20,8,16,256]{3,2,1,0:T(8,128)}, u32[]{:S(2)}) copy-start(f32[20,8,16,256]{3,2,1,0:T(8,128)} %values_ref.1) | copy-start | bytes 7864324
  4.1 70.5 %copy-start.1 = (f32[20,8,16,256]{3,2,1,0:T(8,128)S(1)}, f32[20,8,16,256]{3,2,1,0:T(8,128)}, u32[]{:S(2)}) copy-start(f32[20,8,16,256]{3,2,1,0:T(8,128)} %cot_ref.1) | copy-start | bytes 7864324
  4.1 70.5 %copy-start.3 = (bf16[128,256]{1,0:T(8,128)(2,1)S(1)}, bf16[128,256]{1,0:T(8,128)(2,1)}, u32[]{:S(2)}) copy-start(bf16[128,256]{1,0:T(8,128)(2,1)} %constant.16.clone.back_ref) | copy-start | bytes 196612
  4.1 70.4 %copy-start.8 = (f32[20,20]{1,0:T(8,128)S(1)}, f32[20,20]{1,0:T(8,128)}, u32[]{:S(2)}) copy-start(f32[20,20]{1,0:T(8,128)} %bypass_ref.3) | copy-start | bytes 4804
  4.2 70.4 %copy-start.9 = (f32[20]{0:T(128)S(1)}, f32[20]{0:T(128)}, u32[]{:S(2)}) copy-start(f32[20]{0:T(128)} %bias_hbm.1) | copy-start | bytes 244
  80.1 26.4 %copy-start.2 = (bf16[5120,128]{1,0:T(8,128)(2,1)S(1)}, bf16[5120,128]{1,0:T(8,128)(2,1)}, u32[]{:S(2)}) copy-start(bf16[5120,128]{1,0:T(8,128)(2,1)} %constant.19.clone.join_ref) | copy-start | bytes 3932164

commit v3 on v2

--- a/solution.py
+++ b/solution.py
@@ -352,18 +352,27 @@
     return jnp.concatenate(rows, 0)
 
 
-def lat_forward(lat, block):
-    both = dot3(lat, split(block))
+def stacked(value):
+    high, low = split(value)
+    return jnp.concatenate([high, high, low], 0)
+
+
+def lat_forward(lat_ref, block):
+    both = dot(lat_ref[...], stacked(block))
     return both[:32] - times_i(both[32:])
 
 
-def lat_inverse(lat_back, modes):
-    return dot3(lat_back, split(jnp.concatenate([modes, times_i(modes)], 0)))
-
-
-def spread(modes, lane):
-    left = lane_index(modes.shape) < 64
-    return jnp.where(left, modes[:, lane : lane + 1], modes[:, 64 + lane : 65 + lane])
+def lat_inverse(back_ref, modes):
+    return dot(back_ref[...], stacked(jnp.concatenate([modes, times_i(modes)], 0)))
+
+
+def spread_table():
+    table = np.zeros((128, C, 2, 128))
+    for c in range(C):
+        for part in range(2):
+            for low in range(2):
+                table[64 * low + C * part + c, c, part, 64 * low : 64 * low + 64] = 1
+    return table.reshape(128, 2 * 128 * C)
 
 
 SCALING = 1.0 / math.sqrt(NX * NY * NZ)
@@ -378,25 +387,28 @@
 
 
 def mix_kernel(
-    lat_h, lat_l, back_h, back_l, block_ref, first_ref, out_ref, modes_ref, weights_ref
+    lat_ref, inverse_ref, spread_ref, block_ref, first_ref, out_ref, modes_ref, weights_ref
 ):
-    modes = lat_forward((lat_h[...], lat_l[...]), block_ref[...]) * SCALING
+    modes = lat_forward(lat_ref, block_ref[...]) * SCALING
     modes_ref[...] = modes
+    both = dot(jnp.concatenate(split(modes), 0), spread_ref[...])
+    wide = both[:32] + both[32:]
     direct = jnp.zeros((32, 128), f32)
     crossed = jnp.zeros((32, 128), f32)
     for c in range(C):
         weight = unpack(first_ref, c)
         weights_ref[c] = weight
-        direct = direct + spread(modes, c) * weight
-        crossed = crossed + spread(modes, C + c) * weight
+        at = 256 * c
+        direct = direct + wide[:, at : at + 128] * weight
+        crossed = crossed + wide[:, at + 128 : at + 256] * weight
     mixed = (direct + times_i(crossed)) * depth_factor()
-    out_ref[...] = lat_inverse((back_h[...], back_l[...]), mixed)
-
-
-def mix_call(lat, block, first):
+    out_ref[...] = lat_inverse(inverse_ref, mixed)
+
+
+def mix_call(lat, spreads, block, first):
     return pl.pallas_call(
         mix_kernel,
-        in_specs=[vmem()] * 6,
+        in_specs=[vmem()] * 5,
         out_specs=[vmem()] * 3,
         out_shape=[
             jax.ShapeDtypeStruct((NY, 128), f32),
@@ -404,7 +416,7 @@
             jax.ShapeDtypeStruct((C, 32, 128), f32),
         ],
         compiler_params=params(),
-    )(*lat, block, first)
+    )(*lat, spreads, block, first)
 
 
 def join_table():
@@ -417,9 +429,9 @@
 
 
 def adjoint_kernel(
-    lat_h, lat_l, back_h, back_l, join_ref, block_ref, weights_ref, out_ref, grad_ref
+    lat_ref, inverse_ref, join_ref, block_ref, weights_ref, out_ref, grad_ref
 ):
-    grad = lat_forward((lat_h[...], lat_l[...]), block_ref[...]) * depth_factor()
+    grad = lat_forward(lat_ref, block_ref[...]) * depth_factor()
     grad_ref[...] = grad
     crossed = -times_i(grad)
     terms = []
@@ -429,13 +441,13 @@
     high, low = split(jnp.concatenate(terms, 1))
     both = dot(jnp.concatenate([high, low], 0), join_ref[...])
     block = both[:32] + both[32:]
-    out_ref[...] = lat_inverse((back_h[...], back_l[...]), block * SCALING)
+    out_ref[...] = lat_inverse(inverse_ref, block * SCALING)
 
 
 def adjoint_call(lat, joins, block, weights):
     return pl.pallas_call(
         adjoint_kernel,
-        in_specs=[vmem()] * 7,
+        in_specs=[vmem()] * 5,
         out_specs=[vmem()] * 2,
         out_shape=[
             jax.ShapeDtypeStruct((NY, 128), f32),
@@ -637,13 +649,18 @@
     tables = jnp.asarray(tables)
     joins = jnp.asarray(join_table().astype(ml_dtypes.bfloat16))
     lat_full = lat_table()
-    lat = tuple(jnp.asarray(t) for t in halves(lat_full) + halves(lat_full.T.copy()))
+    lat = tuple(
+        jnp.asarray(np.concatenate([high, low, high], 1))
+        for high, low in (halves(lat_full), halves(lat_full.T.copy()))
+    )
+    spreads = jnp.asarray(spread_table().astype(ml_dtypes.bfloat16))
+
     weights = jnp.transpose(spectral_weights, (0, 2, 3, 4, 5, 1)).reshape(C, 8, MODES, C)
     values = grid_values.reshape(C, LANES, NX)
 
     sent, deep, tables = first_call(deep, tables, values, weights)
     first = exchange(sent, "gz")
-    rows, modes, mixing = mix_call(lat, over_y(join_call(first)), first)
+    rows, modes, mixing = mix_call(lat, spreads, over_y(join_call(first)), first)
     got = gather(fork_call(over_y(rows)))
     output, slopes, sent = layer_call(
         back, deep, tables, bypass_weight, bias_vector, got, grid_values, cotangent

time: 141 us -> 141 us (level)
  no operation moved by 1% of the time
where the time goes in v3:
time: 141 us
  blocking collectives  125 us (89%)
  Pallas kernels  15 us (11%)
    all_to_all x6, blocking collectives, exchange(): return lax.all_to_all(block, axis, split_axis=0, concat_axis=0, tiled=True)  91.2 us
    all_gather x2, blocking collectives, gather(): return lax.all_gather(block, 'gz', axis=0, tiled=True)  33.7 us
    pallas_call x1, Pallas kernels, layer_call(): pl.pallas_call(layer_kernel, in_specs=[vmem()] * 4 + [anywhere()] + [vmem...  5.46 us
    pallas_call x1, Pallas kernels, last_call(): pl.pallas_call(last_kernel, in_specs=[vmem()] * 5, out_specs=[anywhere(),...  3.5 us
    pallas_call x1, Pallas kernels, first_call(): pl.pallas_call(first_kernel, in_specs=[pl.BlockSpec(memory_space=pltpu.HB...  3.45 us

profile of v3, /device:TPU:1, one launch (start us, length us, event | category | flops | bytes accessed | tf_op | source)
XLA Modules:
  0.0 140.9 jit_solution(6827206651718955945)
XLA Ops:
  0.6 0.0 copy-start.6
  0.6 3.4 %shard_map.139 = (f32[8,216,128]{2,1,0:T(8,128)S(1)}, bf16[512,384]{1,0:T(8,128)(2,1)S(1)}, bf16[512,128]{1,0:T(8,128)(2,1)S(1)}) custom-call(bf16[8,512,384]{2,1,0:T(8,128)(2,1)} %constant.15.clone.deep_hbm, bf16[512,128]{1,0:T(8,128)(2,1)} %constant.16.clone.tables_hbm, f32[20,128,256]{2,1,0:T(8,128)} %bitcast.17, f32[20,8,16,20]{3,2,1,0:T(8,128)} %bitcast.26), custom_call_target="tpu_custom_call" | custom-call | tf_op jit(solution)/shard_map/pallas_call | solution.py:249
  4.1 0.0 copy-start.2
  4.1 0.0 copy-start.4
  4.1 0.0 copy-start.5
  4.1 0.0 copy-start.1
  4.1 19.4 %all_to_all.30.block_ref.first_ref = f32[8,216,128]{2,1,0:T(8,128)S(1)} all-to-all(f32[8,216,128]{2,1,0:T(8,128)S(1)} %get-tuple-element.18), channel_id=1, replica_groups=mesh['gy'=32,'gz'=8] {'gz'}, dimensions={0} | all-to-all | bytes 1769472 | tf_op jit(solution)/shard_map/all_to_all | solution.py:627
  23.5 0.0 copy-start
  23.5 0.0 copy-start.7
  23.5 0.0 copy-start.8
  23.5 0.2 shard_map.140
  23.8 20.3 %all_to_all.31 = f32[32,8,128]{2,1,0:T(8,128)S(1)} all-to-all(f32[32,8,128]{2,1,0:T(8,128)S(1)} %bitcast.22), channel_id=1, replica_groups=mesh['gy'=32,'gz'=8] {'gy'}, dimensions={0} | all-to-all | bytes 262144 | tf_op jit(solution)/shard_map/all_to_all | solution.py:627
  44.0 0.0 copy-done.2
  44.0 0.0 copy-done.4
  44.0 0.0 copy-done.5
  44.0 0.9 shard_map.141
  44.9 12.7 %all_to_all.32 = f32[32,8,128]{2,1,0:T(8,128)S(1)} all-to-all(f32[32,8,128]{2,1,0:T(8,128)S(1)} %bitcast.25), channel_id=1, replica_groups=mesh['gy'=32,'gz'=8] {'gy'}, dimensions={0} | all-to-all | bytes 262144 | tf_op jit(solution)/shard_map/all_to_all | solution.py:627
  57.7 0.2 shard_map.142
  57.9 16.5 %all_gather.6.block_ref = f32[8,160,128]{2,1,0:T(8,128)S(1)} all-gather(f32[1,160,128]{2,1,0:T(8,128)S(1)} %shard_map.142), channel_id=1, replica_groups=mesh['gy'=32,'gz'=8] {'gz'}, dimensions={0}, use_global_device_ids=true | all-gather | bytes 737280 | tf_op jit(solution)/shard_map/all_gather | solution.py:631
  74.4 0.0 copy-done.6
  74.4 0.0 copy-done.1
  74.4 0.0 copy-done
  74.4 0.0 copy-done.7
  74.4 0.0 copy-done.8
  74.4 5.5 %shard_map.143 = (f32[20,8,16,256]{3,2,1,0:T(8,128)}, f32[20,8,16,256]{3,2,1,0:T(8,128)S(1)}, f32[8,160,128]{2,1,0:T(8,128)S(1)}) custom-call(bf16[128,256]{1,0:T(8,128)(2,1)S(1)} %copy-done.6, bf16[512,384]{1,0:T(8,128)(2,1)S(1)} %get-tuple-element.16.deep, bf16[512,128]{1,0:T(8,128)(2,1)S(1)} %get-tuple-element.17.tables_ref, f32[20,20]{1,0:T(8,128)S(1)} %copy-done.7, ...), custom_call_target="tpu_custom_call" | custom-call | tf_op jit(solution)/shard_map/pallas_call | solution.py:539
  79.9 0.0 copy-start.3
  79.9 13.8 %all_to_all.33.block_ref = f32[8,160,128]{2,1,0:T(8,128)S(1)} all-to-all(f32[8,160,128]{2,1,0:T(8,128)S(1)} %get-tuple-element.21), channel_id=1, replica_groups=mesh['gy'=32,'gz'=8] {'gz'}, dimensions={0} | all-to-all | bytes 1310720 | tf_op jit(solution)/shard_map/all_to_all | solution.py:627
  93.7 0.2 shard_map.144
  93.9 12.4 %all_to_all.34 = f32[32,8,128]{2,1,0:T(8,128)S(1)} all-to-all(f32[32,8,128]{2,1,0:T(8,128)S(1)} %bitcast.21), channel_id=1, replica_groups=mesh['gy'=32,'gz'=8] {'gy'}, dimensions={0} | all-to-all | bytes 262144 | tf_op jit(solution)/shard_map/all_to_all | solution.py:627
  106.2 0.0 copy-done.3
  106.2 0.9 shard_map.145
  107.1 12.7 %all_to_all.35 = f32[32,8,128]{2,1,0:T(8,128)S(1)} all-to-all(f32[32,8,128]{2,1,0:T(8,128)S(1)} %bitcast.24), channel_id=1, replica_groups=mesh['gy'=32,'gz'=8] {'gy'}, dimensions={0} | all-to-all | bytes 262144 | tf_op jit(solution)/shard_map/all_to_all | solution.py:627
  119.8 0.2 shard_map.146
  120.0 17.2 %all_gather.7.block_ref = f32[8,224,128]{2,1,0:T(8,128)S(1)} all-gather(f32[1,224,128]{2,1,0:T(8,128)S(1)} %shard_map.146), channel_id=1, replica_groups=mesh['gy'=32,'gz'=8] {'gz'}, dimensions={0}, use_global_device_ids=true | all-gather | bytes 1032192 | tf_op jit(solution)/shard_map/all_gather | solution.py:631
  137.2 3.5 %shard_map.147 = (f32[20,8,16,256]{3,2,1,0:T(8,128)}, f32[20,8,16,20]{3,2,1,0:T(8,128)}) custom-call(bf16[128,256]{1,0:T(8,128)(2,1)S(1)} %copy-done.6, bf16[512,384]{1,0:T(8,128)(2,1)S(1)} %get-tuple-element.16.deep, f32[20,20]{1,0:T(8,128)S(1)} %copy-done.7, f32[8,224,128]{2,1,0:T(8,128)S(1)} %all_gather.7.block_ref, ...), custom_call_target="tpu_custom_call" | custom-call | tf_op jit(solution)/shard_map/pallas_call | solution.py:607
Async XLA Ops:
  0.6 73.7 %copy-start.6 = (bf16[128,256]{1,0:T(8,128)(2,1)S(1)}, bf16[128,256]{1,0:T(8,128)(2,1)}, u32[]{:S(2)}) copy-start(bf16[128,256]{1,0:T(8,128)(2,1)} %constant.14.clone.back_ref) | copy-start | bytes 196612
  4.1 39.9 %copy-start.2 = (bf16[128,5120]{1,0:T(8,128)(2,1)S(1)}, bf16[128,5120]{1,0:T(8,128)(2,1)}, u32[]{:S(2)}) copy-start(bf16[128,5120]{1,0:T(8,128)(2,1)} %constant.20.clone.spread_ref) | copy-start | bytes 3932164
  4.1 39.9 %copy-start.4 = (bf16[256,192]{1,0:T(8,128)(2,1)S(1)}, bf16[256,192]{1,0:T(8,128)(2,1)}, u32[]{:S(2)}) copy-start(bf16[256,192]{1,0:T(8,128)(2,1)} %constant.19.clone.inverse_ref) | copy-start | bytes 294916
  4.1 39.9 %copy-start.5 = (bf16[64,768]{1,0:T(8,128)(2,1)S(1)}, bf16[64,768]{1,0:T(8,128)(2,1)}, u32[]{:S(2)}) copy-start(bf16[64,768]{1,0:T(8,128)(2,1)} %constant.18.clone.lat_ref) | copy-start | bytes 294916
  4.1 70.2 %copy-start.1 = (f32[20,8,16,256]{3,2,1,0:T(8,128)S(1)}, f32[20,8,16,256]{3,2,1,0:T(8,128)}, u32[]{:S(2)}) copy-start(f32[20,8,16,256]{3,2,1,0:T(8,128)} %cot_ref.1) | copy-start | bytes 7864324
  23.5 50.9 %copy-start = (f32[20,8,16,256]{3,2,1,0:T(8,128)S(1)}, f32[20,8,16,256]{3,2,1,0:T(8,128)}, u32[]{:S(2)}) copy-start(f32[20,8,16,256]{3,2,1,0:T(8,128)} %values_ref.1) | copy-start | bytes 7864324
  23.5 50.9 %copy-start.7 = (f32[20,20]{1,0:T(8,128)S(1)}, f32[20,20]{1,0:T(8,128)}, u32[]{:S(2)}) copy-start(f32[20,20]{1,0:T(8,128)} %bypass_ref.3) | copy-start | bytes 4804
  23.5 50.9 %copy-start.8 = (f32[20]{0:T(128)S(1)}, f32[20]{0:T(128)}, u32[]{:S(2)}) copy-start(f32[20]{0:T(128)} %bias_hbm.1) | copy-start | bytes 244
  79.9 26.4 %copy-start.3 = (bf16[5120,128]{1,0:T(8,128)(2,1)S(1)}, bf16[5120,128]{1,0:T(8,128)(2,1)}, u32[]{:S(2)}) copy-start(bf16[5120,128]{1,0:T(8,128)(2,1)} %constant.17.clone.join_ref) | copy-start | bytes 3932164

commit v4 on v3

--- a/solution.py
+++ b/solution.py
@@ -207,10 +207,11 @@
 
 
 def first_kernel(
-    deep_hbm, tables_hbm, values_hbm, weights_hbm, out_ref, deep, tables, values, weights, coef,
-    sems
+    deep_hbm, tables_hbm, values_hbm, weights_hbm, bypass_hbm, out_ref, deep, tables, ahead_ref,
+    back_ref, values, weights, bypass, coef, sems
 ):
     fetch = Fetch(sems)
+    bypass_copy = fetch.start(bypass_hbm, bypass)
     tables_copy = fetch.start(tables_hbm, tables)
     copies = []
     for k in range(STEPS):
@@ -219,6 +220,9 @@
     deep_copy = fetch_deep(fetch, deep_hbm, deep)
     weights_copy = fetch.start(weights_hbm, weights)
     clear_extra(coef)
+    bypass_copy.wait()
+    ahead_ref[...] = bypass_blocks(bypass[...], ((1,), (1,)))
+    back_ref[...] = bypass_blocks(bypass[...], ((1,), (0,)))
     tables_copy.wait()
     for k in range(STEPS):
         copies[k].wait()
@@ -243,23 +247,27 @@
     return pltpu.CompilerParams(vmem_limit_bytes=limit)
 
 
-def first_call(deep, tables, values, weights):
+def first_call(deep, tables, values, weights, bypass):
     shape = (GZ, SEND_ROWS + WEIGHT_ROWS, 128)
-    operands = (deep, tables, values, weights)
+    operands = (deep, tables, values, weights, bypass)
+    blocks = jax.ShapeDtypeStruct((8 * C, 24 * C), bf16)
     return pl.pallas_call(
         first_kernel,
         in_specs=[pl.BlockSpec(memory_space=pltpu.HBM)] * len(operands),
-        out_specs=[vmem()] * 3,
+        out_specs=[vmem()] * 5,
         out_shape=[
             jax.ShapeDtypeStruct(shape, f32),
             jax.ShapeDtypeStruct(deep.shape[1:], bf16),
             jax.ShapeDtypeStruct(tables.shape, bf16),
+            blocks,
+            blocks,
         ],
         scratch_shapes=[
             pltpu.VMEM(values.shape, f32),
             pltpu.VMEM(weights.shape, f32),
+            pltpu.VMEM(bypass.shape, f32),
             pltpu.VMEM((COEF_ROWS, LANES), f32),
-            pltpu.SemaphoreType.DMA((STEPS + 3,)),
+            pltpu.SemaphoreType.DMA((STEPS + 4,)),
         ],
         compiler_params=params(WIDE_LIMIT),
     )(*(pltpu.with_memory_space_constraint(a, pltpu.HBM) for a in operands))
@@ -480,8 +488,7 @@
     return dot(blocks, jnp.concatenate([high, high, low], 0))
 
 
-def bypass_rows(bypass, dims, values_ref, field):
-    blocks = bypass_blocks(bypass, dims)
+def bypass_rows(blocks, values_ref, field):
     for y in range(YL):
         for half in range(2):
             rows = slice(8 * half, 8 * half + 8)
@@ -501,7 +508,7 @@
         group = pl.ds(part * OUT_C, OUT_C)
         return pltpu.make_async_copy(outs.at[group], out_hbm.at[group], sems.at[part])
 
-    bypass_rows(bypass_ref[...], ((1,), (1,)), values_ref, field)
+    bypass_rows(bypass_ref[...], values_ref, field)
     deep_inverse(deep, block_ref, coef)
     bias_copy.wait()
     for step in range(C // PAIR):
@@ -587,7 +594,7 @@
     deep_inverse(deep, block_ref, coef)
     for channel in range(C):
         field[channel] = wide_inverse(coef, back_ref[...], channel)
-    blocks = bypass_blocks(bypass_ref[...], ((1,), (0,)))
+    blocks = bypass_ref[...]
     for y in range(YL):
         for half in range(2):
             rows = slice(8 * half, 8 * half + 8)
@@ -658,18 +665,20 @@
     weights = jnp.transpose(spectral_weights, (0, 2, 3, 4, 5, 1)).reshape(C, 8, MODES, C)
     values = grid_values.reshape(C, LANES, NX)
 
-    sent, deep, tables = first_call(deep, tables, values, weights)
+    sent, deep, tables, ahead, behind = first_call(
+        deep, tables, values, weights, bypass_weight
+    )
     first = exchange(sent, "gz")
     rows, modes, mixing = mix_call(lat, spreads, over_y(join_call(first)), first)
     got = gather(fork_call(over_y(rows)))
     output, slopes, sent = layer_call(
-        back, deep, tables, bypass_weight, bias_vector, got, grid_values, cotangent
+        back, deep, tables, ahead, bias_vector, got, grid_values, cotangent
     )
 
     got = exchange(sent, "gz")
     rows, grad = adjoint_call(lat, joins, over_y(join_call(got)), mixing)
     got = gather(fork_call(over_y(rows), modes, grad))
-    grad_values, weight_grad = last_call(back, deep, bypass_weight, got, slopes)
+    grad_values, weight_grad = last_call(back, deep, behind, got, slopes)
     weight_grad = weight_grad.reshape(C, 2, 1, 4, MODES, C)
     return output, grad_values, jnp.transpose(weight_grad, (0, 5, 1, 2, 3, 4))
 

time: 141 us -> 140 us (level)
  no operation moved by 1% of the time
where the time goes in v4:
time: 140 us
  blocking collectives  125 us (89%)
  Pallas kernels  14.5 us (10%)
    all_to_all x6, blocking collectives, exchange(): return lax.all_to_all(block, axis, split_axis=0, concat_axis=0, tiled=True)  91.2 us
    all_gather x2, blocking collectives, gather(): return lax.all_gather(block, 'gz', axis=0, tiled=True)  33.5 us
    pallas_call x1, Pallas kernels, layer_call(): pl.pallas_call(layer_kernel, in_specs=[vmem()] * 4 + [anywhere()] + [vmem...  5.22 us
    pallas_call x1, Pallas kernels, first_call(): pl.pallas_call(first_kernel, in_specs=[pl.BlockSpec(memory_space=pltpu.HB...  3.46 us
    pallas_call x1, Pallas kernels, last_call(): pl.pallas_call(last_kernel, in_specs=[vmem()] * 5, out_specs=[anywhere(),...  3.21 us

profile of v4, /device:TPU:1, one launch (start us, length us, event | category | flops | bytes accessed | tf_op | source)
XLA Modules:
  0.0 140.0 jit_solution(16139977779641266774)
XLA Ops:
  0.6 0.0 copy-start.6
  0.6 3.5 %shard_map.139 = (f32[8,216,128]{2,1,0:T(8,128)S(1)}, bf16[512,384]{1,0:T(8,128)(2,1)S(1)}, bf16[512,128]{1,0:T(8,128)(2,1)S(1)}, bf16[160,480]{1,0:T(8,128)(2,1)S(1)}, bf16[160,480]{1,0:T(8,128)(2,1)S(1)}) custom-call(bf16[8,512,384]{2,1,0:T(8,128)(2,1)} %constant.15.clone.deep_hbm, bf16[512,128]{1,0:T(8,128)(2,1)} %constant.16.clone.tables_hbm, ...), custom_call_target="tpu_custom_call" | custom-call | tf_op jit(solution)/shard_map/pallas_call | solution.py:254
  4.1 0.0 copy-start.2
  4.1 0.0 copy-start.4
  4.1 0.0 copy-start.5
  4.1 0.0 copy-start.1
  4.2 19.4 %all_to_all.30.block_ref.first_ref = f32[8,216,128]{2,1,0:T(8,128)S(1)} all-to-all(f32[8,216,128]{2,1,0:T(8,128)S(1)} %get-tuple-element.21), channel_id=1, replica_groups=mesh['gy'=32,'gz'=8] {'gz'}, dimensions={0} | all-to-all | bytes 1769472 | tf_op jit(solution)/shard_map/all_to_all | solution.py:634
  23.5 0.0 copy-start
  23.5 0.0 copy-start.7
  23.5 0.2 shard_map.140
  23.8 20.3 %all_to_all.31 = f32[32,8,128]{2,1,0:T(8,128)S(1)} all-to-all(f32[32,8,128]{2,1,0:T(8,128)S(1)} %bitcast.22), channel_id=1, replica_groups=mesh['gy'=32,'gz'=8] {'gy'}, dimensions={0} | all-to-all | bytes 262144 | tf_op jit(solution)/shard_map/all_to_all | solution.py:634
  44.0 0.0 copy-done.2
  44.0 0.0 copy-done.4
  44.0 0.0 copy-done.5
  44.0 0.9 shard_map.141
  44.9 12.7 %all_to_all.32 = f32[32,8,128]{2,1,0:T(8,128)S(1)} all-to-all(f32[32,8,128]{2,1,0:T(8,128)S(1)} %bitcast.25), channel_id=1, replica_groups=mesh['gy'=32,'gz'=8] {'gy'}, dimensions={0} | all-to-all | bytes 262144 | tf_op jit(solution)/shard_map/all_to_all | solution.py:634
  57.7 0.2 shard_map.142
  57.9 16.5 %all_gather.6.block_ref = f32[8,160,128]{2,1,0:T(8,128)S(1)} all-gather(f32[1,160,128]{2,1,0:T(8,128)S(1)} %shard_map.142), channel_id=1, replica_groups=mesh['gy'=32,'gz'=8] {'gz'}, dimensions={0}, use_global_device_ids=true | all-gather | bytes 737280 | tf_op jit(solution)/shard_map/all_gather | solution.py:638
  74.4 0.0 copy-done.6
  74.4 0.0 copy-done.1
  74.4 0.0 copy-done
  74.4 0.0 copy-done.7
  74.4 5.2 %shard_map.143 = (f32[20,8,16,256]{3,2,1,0:T(8,128)}, f32[20,8,16,256]{3,2,1,0:T(8,128)S(1)}, f32[8,160,128]{2,1,0:T(8,128)S(1)}) custom-call(bf16[128,256]{1,0:T(8,128)(2,1)S(1)} %copy-done.6, bf16[512,384]{1,0:T(8,128)(2,1)S(1)} %get-tuple-element.18.deep, bf16[512,128]{1,0:T(8,128)(2,1)S(1)} %get-tuple-element.19.tables_ref, ...), custom_call_target="tpu_custom_call" | custom-call | tf_op jit(solution)/shard_map/pallas_call | solution.py:546
  79.6 0.0 copy-start.3
  79.6 13.8 %all_to_all.33.block_ref = f32[8,160,128]{2,1,0:T(8,128)S(1)} all-to-all(f32[8,160,128]{2,1,0:T(8,128)S(1)} %get-tuple-element.25), channel_id=1, replica_groups=mesh['gy'=32,'gz'=8] {'gz'}, dimensions={0} | all-to-all | bytes 1310720 | tf_op jit(solution)/shard_map/all_to_all | solution.py:634
  93.4 0.2 shard_map.144
  93.6 12.4 %all_to_all.34 = f32[32,8,128]{2,1,0:T(8,128)S(1)} all-to-all(f32[32,8,128]{2,1,0:T(8,128)S(1)} %bitcast.21), channel_id=1, replica_groups=mesh['gy'=32,'gz'=8] {'gy'}, dimensions={0} | all-to-all | bytes 262144 | tf_op jit(solution)/shard_map/all_to_all | solution.py:634
  106.0 0.0 copy-done.3
  106.0 0.9 shard_map.145
  106.9 12.7 %all_to_all.35 = f32[32,8,128]{2,1,0:T(8,128)S(1)} all-to-all(f32[32,8,128]{2,1,0:T(8,128)S(1)} %bitcast.24), channel_id=1, replica_groups=mesh['gy'=32,'gz'=8] {'gy'}, dimensions={0} | all-to-all | bytes 262144 | tf_op jit(solution)/shard_map/all_to_all | solution.py:634
  119.6 0.2 shard_map.146
  119.8 17.0 %all_gather.7.block_ref = f32[8,224,128]{2,1,0:T(8,128)S(1)} all-gather(f32[1,224,128]{2,1,0:T(8,128)S(1)} %shard_map.146), channel_id=1, replica_groups=mesh['gy'=32,'gz'=8] {'gz'}, dimensions={0}, use_global_device_ids=true | all-gather | bytes 1032192 | tf_op jit(solution)/shard_map/all_gather | solution.py:638
  136.8 3.2 %shard_map.147 = (f32[20,8,16,256]{3,2,1,0:T(8,128)}, f32[20,8,16,20]{3,2,1,0:T(8,128)}) custom-call(bf16[128,256]{1,0:T(8,128)(2,1)S(1)} %copy-done.6, bf16[512,384]{1,0:T(8,128)(2,1)S(1)} %get-tuple-element.18.deep, bf16[160,480]{1,0:T(8,128)(2,1)S(1)} %get-tuple-element.24.bypass_ref, f32[8,224,128]{2,1,0:T(8,128)S(1)} %all_gather.7.block_ref, ...), custom_call_target="tpu_custom_call" | custom-call | tf_op jit(solution)/shard_map/pallas_call | solution.py:614
Async XLA Ops:
  0.6 73.8 %copy-start.6 = (bf16[128,256]{1,0:T(8,128)(2,1)S(1)}, bf16[128,256]{1,0:T(8,128)(2,1)}, u32[]{:S(2)}) copy-start(bf16[128,256]{1,0:T(8,128)(2,1)} %constant.14.clone.back_ref) | copy-start | bytes 196612
  4.1 39.9 %copy-start.2 = (bf16[128,5120]{1,0:T(8,128)(2,1)S(1)}, bf16[128,5120]{1,0:T(8,128)(2,1)}, u32[]{:S(2)}) copy-start(bf16[128,5120]{1,0:T(8,128)(2,1)} %constant.20.clone.spread_ref) | copy-start | bytes 3932164
  4.1 39.9 %copy-start.4 = (bf16[256,192]{1,0:T(8,128)(2,1)S(1)}, bf16[256,192]{1,0:T(8,128)(2,1)}, u32[]{:S(2)}) copy-start(bf16[256,192]{1,0:T(8,128)(2,1)} %constant.19.clone.inverse_ref) | copy-start | bytes 294916
  4.1 39.9 %copy-start.5 = (bf16[64,768]{1,0:T(8,128)(2,1)S(1)}, bf16[64,768]{1,0:T(8,128)(2,1)}, u32[]{:S(2)}) copy-start(bf16[64,768]{1,0:T(8,128)(2,1)} %constant.18.clone.lat_ref) | copy-start | bytes 294916
  4.1 70.2 %copy-start.1 = (f32[20,8,16,256]{3,2,1,0:T(8,128)S(1)}, f32[20,8,16,256]{3,2,1,0:T(8,128)}, u32[]{:S(2)}) copy-start(f32[20,8,16,256]{3,2,1,0:T(8,128)} %cot_ref.1) | copy-start | bytes 7864324
  23.5 50.9 %copy-start = (f32[20,8,16,256]{3,2,1,0:T(8,128)S(1)}, f32[20,8,16,256]{3,2,1,0:T(8,128)}, u32[]{:S(2)}) copy-start(f32[20,8,16,256]{3,2,1,0:T(8,128)} %values_ref.1) | copy-start | bytes 7864324
  23.5 50.9 %copy-start.7 = (f32[20]{0:T(128)S(1)}, f32[20]{0:T(128)}, u32[]{:S(2)}) copy-start(f32[20]{0:T(128)} %bias_hbm.1) | copy-start | bytes 244
  79.6 26.4 %copy-start.3 = (bf16[5120,128]{1,0:T(8,128)(2,1)S(1)}, bf16[5120,128]{1,0:T(8,128)(2,1)}, u32[]{:S(2)}) copy-start(bf16[5120,128]{1,0:T(8,128)(2,1)} %constant.17.clone.join_ref) | copy-start | bytes 3932164

commit v5 on v4

--- a/solution.py
+++ b/solution.py
@@ -155,9 +155,9 @@
 def deep_inverse(deep_ref, block_ref, coef_ref):
     def product(at, rows):
         high, low = split(rows)
-        table = deep_ref[2 * LANES * at : 2 * LANES * at + 2 * LANES, : 2 * LANES]
-        wide = dot(high, table)
-        return wide[:, :LANES] + wide[:, LANES:] + dot(low, table[:, :LANES])
+        table = deep_ref[2 * LANES * at : 2 * LANES * at + 2 * LANES, :]
+        table = [table[:, LANES * k : LANES * k + LANES] for k in range(3)]
+        return dot(jnp.concatenate([high, high, low], 1), jnp.concatenate(table, 0))
 
     sections = []
     for t in range(TILES):

time: 140 us -> 141 us (level)
  no operation moved by 1% of the time
where the time goes in v5:
time: 141 us
  blocking collectives  125 us (89%)
  Pallas kernels  14.9 us (11%)
    all_to_all x6, blocking collectives, exchange(): return lax.all_to_all(block, axis, split_axis=0, concat_axis=0, tiled=True)  91.2 us
    all_gather x2, blocking collectives, gather(): return lax.all_gather(block, 'gz', axis=0, tiled=True)  33.7 us
    pallas_call x1, Pallas kernels, layer_call(): pl.pallas_call(layer_kernel, in_specs=[vmem()] * 4 + [anywhere()] + [vmem...  5.35 us
    pallas_call x1, Pallas kernels, first_call(): pl.pallas_call(first_kernel, in_specs=[pl.BlockSpec(memory_space=pltpu.HB...  3.46 us
    pallas_call x1, Pallas kernels, last_call(): pl.pallas_call(last_kernel, in_specs=[vmem()] * 5, out_specs=[anywhere(),...  3.44 us

profile of v5, /device:TPU:1, one launch (start us, length us, event | category | flops | bytes accessed | tf_op | source)
XLA Modules:
  0.0 140.7 jit_solution(13095784084615451253)
XLA Ops:
  0.6 0.0 copy-start.6
  0.6 3.5 %shard_map.139 = (f32[8,216,128]{2,1,0:T(8,128)S(1)}, bf16[512,384]{1,0:T(8,128)(2,1)S(1)}, bf16[512,128]{1,0:T(8,128)(2,1)S(1)}, bf16[160,480]{1,0:T(8,128)(2,1)S(1)}, bf16[160,480]{1,0:T(8,128)(2,1)S(1)}) custom-call(bf16[8,512,384]{2,1,0:T(8,128)(2,1)} %constant.15.clone.deep_hbm, bf16[512,128]{1,0:T(8,128)(2,1)} %constant.16.clone.tables_hbm, ...), custom_call_target="tpu_custom_call" | custom-call | tf_op jit(solution)/shard_map/pallas_call | solution.py:254
  4.1 0.0 copy-start.2
  4.1 0.0 copy-start.4
  4.1 0.0 copy-start.5
  4.1 0.0 copy-start.1
  4.2 19.4 %all_to_all.30.block_ref.first_ref = f32[8,216,128]{2,1,0:T(8,128)S(1)} all-to-all(f32[8,216,128]{2,1,0:T(8,128)S(1)} %get-tuple-element.21), channel_id=1, replica_groups=mesh['gy'=32,'gz'=8] {'gz'}, dimensions={0} | all-to-all | bytes 1769472 | tf_op jit(solution)/shard_map/all_to_all | solution.py:634
  23.5 0.0 copy-start
  23.5 0.0 copy-start.7
  23.5 0.2 shard_map.140
  23.8 20.3 %all_to_all.31 = f32[32,8,128]{2,1,0:T(8,128)S(1)} all-to-all(f32[32,8,128]{2,1,0:T(8,128)S(1)} %bitcast.22), channel_id=1, replica_groups=mesh['gy'=32,'gz'=8] {'gy'}, dimensions={0} | all-to-all | bytes 262144 | tf_op jit(solution)/shard_map/all_to_all | solution.py:634
  44.0 0.0 copy-done.2
  44.0 0.0 copy-done.4
  44.0 0.0 copy-done.5
  44.0 0.9 shard_map.141
  44.9 12.7 %all_to_all.32 = f32[32,8,128]{2,1,0:T(8,128)S(1)} all-to-all(f32[32,8,128]{2,1,0:T(8,128)S(1)} %bitcast.25), channel_id=1, replica_groups=mesh['gy'=32,'gz'=8] {'gy'}, dimensions={0} | all-to-all | bytes 262144 | tf_op jit(solution)/shard_map/all_to_all | solution.py:634
  57.7 0.2 shard_map.142
  57.9 16.5 %all_gather.6.block_ref = f32[8,160,128]{2,1,0:T(8,128)S(1)} all-gather(f32[1,160,128]{2,1,0:T(8,128)S(1)} %shard_map.142), channel_id=1, replica_groups=mesh['gy'=32,'gz'=8] {'gz'}, dimensions={0}, use_global_device_ids=true | all-gather | bytes 737280 | tf_op jit(solution)/shard_map/all_gather | solution.py:638
  74.4 0.0 copy-done.6
  74.4 0.0 copy-done.1
  74.4 0.0 copy-done
  74.4 0.0 copy-done.7
  74.4 5.3 %shard_map.143 = (f32[20,8,16,256]{3,2,1,0:T(8,128)}, f32[20,8,16,256]{3,2,1,0:T(8,128)S(1)}, f32[8,160,128]{2,1,0:T(8,128)S(1)}) custom-call(bf16[128,256]{1,0:T(8,128)(2,1)S(1)} %copy-done.6, bf16[512,384]{1,0:T(8,128)(2,1)S(1)} %get-tuple-element.18.deep, bf16[512,128]{1,0:T(8,128)(2,1)S(1)} %get-tuple-element.19.tables_ref, ...), custom_call_target="tpu_custom_call" | custom-call | tf_op jit(solution)/shard_map/pallas_call | solution.py:546
  79.8 0.0 copy-start.3
  79.8 13.8 %all_to_all.33.block_ref = f32[8,160,128]{2,1,0:T(8,128)S(1)} all-to-all(f32[8,160,128]{2,1,0:T(8,128)S(1)} %get-tuple-element.25), channel_id=1, replica_groups=mesh['gy'=32,'gz'=8] {'gz'}, dimensions={0} | all-to-all | bytes 1310720 | tf_op jit(solution)/shard_map/all_to_all | solution.py:634
  93.6 0.2 shard_map.144
  93.8 12.4 %all_to_all.34 = f32[32,8,128]{2,1,0:T(8,128)S(1)} all-to-all(f32[32,8,128]{2,1,0:T(8,128)S(1)} %bitcast.21), channel_id=1, replica_groups=mesh['gy'=32,'gz'=8] {'gy'}, dimensions={0} | all-to-all | bytes 262144 | tf_op jit(solution)/shard_map/all_to_all | solution.py:634
  106.1 0.0 copy-done.3
  106.1 0.9 shard_map.145
  107.0 12.7 %all_to_all.35 = f32[32,8,128]{2,1,0:T(8,128)S(1)} all-to-all(f32[32,8,128]{2,1,0:T(8,128)S(1)} %bitcast.24), channel_id=1, replica_groups=mesh['gy'=32,'gz'=8] {'gy'}, dimensions={0} | all-to-all | bytes 262144 | tf_op jit(solution)/shard_map/all_to_all | solution.py:634
  119.8 0.2 shard_map.146
  120.0 17.2 %all_gather.7.block_ref = f32[8,224,128]{2,1,0:T(8,128)S(1)} all-gather(f32[1,224,128]{2,1,0:T(8,128)S(1)} %shard_map.146), channel_id=1, replica_groups=mesh['gy'=32,'gz'=8] {'gz'}, dimensions={0}, use_global_device_ids=true | all-gather | bytes 1032192 | tf_op jit(solution)/shard_map/all_gather | solution.py:638
  137.1 3.4 %shard_map.147 = (f32[20,8,16,256]{3,2,1,0:T(8,128)}, f32[20,8,16,20]{3,2,1,0:T(8,128)}) custom-call(bf16[128,256]{1,0:T(8,128)(2,1)S(1)} %copy-done.6, bf16[512,384]{1,0:T(8,128)(2,1)S(1)} %get-tuple-element.18.deep, bf16[160,480]{1,0:T(8,128)(2,1)S(1)} %get-tuple-element.24.bypass_ref, f32[8,224,128]{2,1,0:T(8,128)S(1)} %all_gather.7.block_ref, ...), custom_call_target="tpu_custom_call" | custom-call | tf_op jit(solution)/shard_map/pallas_call | solution.py:614
Async XLA Ops:
  0.6 73.8 %copy-start.6 = (bf16[128,256]{1,0:T(8,128)(2,1)S(1)}, bf16[128,256]{1,0:T(8,128)(2,1)}, u32[]{:S(2)}) copy-start(bf16[128,256]{1,0:T(8,128)(2,1)} %constant.14.clone.back_ref) | copy-start | bytes 196612
  4.1 39.9 %copy-start.2 = (bf16[128,5120]{1,0:T(8,128)(2,1)S(1)}, bf16[128,5120]{1,0:T(8,128)(2,1)}, u32[]{:S(2)}) copy-start(bf16[128,5120]{1,0:T(8,128)(2,1)} %constant.20.clone.spread_ref) | copy-start | bytes 3932164
  4.1 39.9 %copy-start.4 = (bf16[256,192]{1,0:T(8,128)(2,1)S(1)}, bf16[256,192]{1,0:T(8,128)(2,1)}, u32[]{:S(2)}) copy-start(bf16[256,192]{1,0:T(8,128)(2,1)} %constant.19.clone.inverse_ref) | copy-start | bytes 294916
  4.1 39.9 %copy-start.5 = (bf16[64,768]{1,0:T(8,128)(2,1)S(1)}, bf16[64,768]{1,0:T(8,128)(2,1)}, u32[]{:S(2)}) copy-start(bf16[64,768]{1,0:T(8,128)(2,1)} %constant.18.clone.lat_ref) | copy-start | bytes 294916
  4.1 70.3 %copy-start.1 = (f32[20,8,16,256]{3,2,1,0:T(8,128)S(1)}, f32[20,8,16,256]{3,2,1,0:T(8,128)}, u32[]{:S(2)}) copy-start(f32[20,8,16,256]{3,2,1,0:T(8,128)} %cot_ref.1) | copy-start | bytes 7864324
  23.5 50.9 %copy-start = (f32[20,8,16,256]{3,2,1,0:T(8,128)S(1)}, f32[20,8,16,256]{3,2,1,0:T(8,128)}, u32[]{:S(2)}) copy-start(f32[20,8,16,256]{3,2,1,0:T(8,128)} %values_ref.1) | copy-start | bytes 7864324
  23.5 50.9 %copy-start.7 = (f32[20]{0:T(128)S(1)}, f32[20]{0:T(128)}, u32[]{:S(2)}) copy-start(f32[20]{0:T(128)} %bias_hbm.1) | copy-start | bytes 244
  79.8 26.4 %copy-start.3 = (bf16[5120,128]{1,0:T(8,128)(2,1)S(1)}, bf16[5120,128]{1,0:T(8,128)(2,1)}, u32[]{:S(2)}) copy-start(bf16[5120,128]{1,0:T(8,128)(2,1)} %constant.17.clone.join_ref) | copy-start | bytes 3932164
